TPU v7x, 256 devices: a whole 4x4x8 slice. The times are simulated.
256 devices in a mesh: row: 32 (over y, x, core), col: 8 (over z).
Axes of the slice: x: 4, y: 4, z: 8, core: 2. Of those that a mesh axis runs over, the one named last changes fastest.
Arguments:
- x_state: float32 [64, 262144], P(None, ('row', 'col')), may hold values from -6 to 6
- p_state: float32 [64, 262144], P(None, ('row', 'col')), may hold values from -6 to 6
- ax_state: float32 [64, 262144], P(None, ('row', 'col')), may hold values from -27 to 27
- ap_state: float32 [64, 262144], P(None, ('row', 'col')), may hold values from -27 to 27
- stiff_diag: float32 [64, 262144], P(None, ('row', 'col')), may hold values from 1 to 72
- tiles: float32 [64, 9437184], P(None, ('row', 'col')), may hold values from -0.1875 to 0.1875
- tile_rows: int32 [147456], P(('row', 'col')), may hold values from 0 to 47, as said below
- tile_cols: int32 [147456], P(('row', 'col')), may hold values from 0 to 127
- tile_count: int32 [256], P(('row', 'col')), may hold values from 144 to 576, as said below
- rotation: float32 [2, 192, 64], replicated, may hold values from -1.5 to 1.5
Outputs:
- next_x: float32 [64, 262144], P(None, ('row', 'col'))
- next_p: float32 [64, 262144], P(None, ('row', 'col'))
- next_ax: float32 [64, 262144], P(None, ('row', 'col'))
- next_ap: float32 [64, 262144], P(None, ('row', 'col'))
- grams: float32 [2, 2, 192, 192], replicated
Inputs may be any that keep to these rules, and one draw needn't show every extreme that they name: `tile_rows`: the devices with row index 0 have no slot with local row under 16, those with the last row index none at 32 or over. `tile_count`: values of slots at or past a device's count are to be ignored; some device is full.
All inputs are finite; a program needn't handle non-finite values.
Results may differ from a plain program's by a relative error of at most 0.0003.
Values sent between devices are 32-bit elements; how exact they have to be, the bound alone decides.
A program may use at most 192 MiB of HBM per device.

v0:
```python
import jax
import jax.numpy as jnp
from jax import lax
from jax.sharding import PartitionSpec as P

PRECISION_TOP = lax.Precision.HIGHEST


def passed_along(value, axis, steps):
    count = lax.axis_size(axis)
    initial, last = (max(0, -steps), min(count, count - steps))
    return lax.ppermute(value, axis, [(source, source + steps) for source in range(initial, last)])


def apply_stiffness(field, tiles, tile_rows, tile_cols, tile_count, stiff_diag):
    modes, local = field.shape
    slots = tile_rows.shape[0]
    width = tiles.shape[0]
    blocks = local // width
    gathered = lax.all_gather(field, "col", axis=1, tiled=True)
    picked = gathered.reshape(modes, -1, width)[:, tile_cols, :]
    slabs = tiles.reshape(width, slots, width)
    matrix_product = jnp.einsum("mte,ate->mta", picked, slabs, precision=PRECISION_TOP)
    live = (jnp.arange(slots, dtype=jnp.int32) < tile_count[0]).astype(jnp.float32)
    select_entries = (
        tile_rows[:, None] == jnp.arange(3 * blocks, dtype=jnp.int32)[None, :]
    ).astype(jnp.float32)
    select_entries = select_entries * live[:, None]
    partial_result_value = jnp.einsum(
        "fnx,nj->fjx", matrix_product, select_entries, precision=PRECISION_TOP
    ).reshape(modes, 3 * local)
    from_below = passed_along(partial_result_value[:, 2 * local :], "row", 1)
    from_above = passed_along(partial_result_value[:, :local], "row", -1)
    summed = partial_result_value[:, local : 2 * local] + from_below + from_above
    return summed + stiff_diag * field


def body(
    x_state,
    p_state,
    ax_state,
    ap_state,
    stiff_diag,
    tiles,
    tile_rows,
    tile_cols,
    tile_count,
    rotation,
):
    modes = x_state.shape[0]
    total = x_state.shape[1] * lax.axis_size("row") * lax.axis_size("col")
    modes_now, search_now = (x_state, p_state)
    image_now, search_image = (ax_state, ap_state)
    grams_all = []
    for step in range(rotation.shape[0]):
        local_block = jnp.einsum("mn,kn->mk", modes_now, image_now, precision=PRECISION_TOP)
        rayleigh_block = lax.psum(local_block, ("row", "col")) / total
        residual = image_now - jnp.einsum(
            "mk,mn->kn", rayleigh_block, modes_now, precision=PRECISION_TOP
        )
        correction = residual / stiff_diag
        correction_image = apply_stiffness(
            correction, tiles, tile_rows, tile_cols, tile_count, stiff_diag
        )
        basis = jnp.concatenate([modes_now, correction, search_now], axis=0)
        basis_stiff_image = jnp.concatenate([image_now, correction_image, search_image], axis=0)
        local_a = jnp.einsum("kn,ln->kl", basis, basis_stiff_image, precision=PRECISION_TOP)
        local_b = jnp.einsum("kn,ln->kl", basis, basis, precision=PRECISION_TOP)
        gram_a, gram_b = lax.psum((local_a, local_b), ("row", "col"))
        gram_a = gram_a / total
        gram_b = gram_b / total
        grams_all.append(jnp.stack([gram_a, gram_b]))
        rotation_now = rotation[step]
        modes_now = jnp.einsum("kj,kn->jn", rotation_now, basis, precision=PRECISION_TOP)
        image_now = jnp.einsum(
            "kj,kn->jn", rotation_now, basis_stiff_image, precision=PRECISION_TOP
        )
        search_now = jnp.einsum(
            "kj,kn->jn", rotation_now[modes:], basis[modes:], precision=PRECISION_TOP
        )
        search_image = jnp.einsum(
            "kj,kn->jn", rotation_now[modes:], basis_stiff_image[modes:], precision=PRECISION_TOP
        )
    return (modes_now, search_now, image_now, search_image, jnp.stack(grams_all))


def solution(mesh):
    placed = (
        P(None, ("row", "col")),
        P(None, ("row", "col")),
        P(None, ("row", "col")),
        P(None, ("row", "col")),
        P(None, ("row", "col")),
        P(None, ("row", "col")),
        P(("row", "col")),
        P(("row", "col")),
        P(("row", "col")),
        P(),
    )
    return jax.shard_map(
        body,
        mesh=mesh,
        in_specs=placed,
        out_specs=(
            P(None, ("row", "col")),
            P(None, ("row", "col")),
            P(None, ("row", "col")),
            P(None, ("row", "col")),
            P(),
        ),
        check_vma=False,
    )
```

profile of v0, /device:TPU:1, one launch (start us, length us, event | category | flops | bytes accessed | tf_op | source)
XLA Modules:
  0.0 734.8 jit_solution(17968375364191916485)
XLA Ops:
  7.2 1.4 fusion.87
  8.6 81.5 %psum.42 = f32[64,64]{1,0:T(8,128)S(1)} all-reduce(f32[64,64]{1,0:T(8,128)S(1)} %fusion.87), channel_id=1, replica_groups=mesh['row'=32,'col'=8] {'row','col'}, use_global_device_ids=true, to_apply=%region_0.0 | all-reduce | flops 4096 | bytes 32768 | tf_op jit(solution)/shard_map/psum | solution.py:57
  90.1 2.2 fusion.15
  92.4 0.0 all-gather.5.cloned.1.call-start
  92.4 13.8 %copy.20 = f32[64,36864]{0,1:T(8,128)} copy(f32[64,36864]{1,0:T(8,128)} %param.15) | data formatting | bytes 18874368 | tf_op jit(solution)/shard_map/reshape | solution.py:22
  106.9 18.3 %all-gather.3.cloned.1.call-done = f32[64,8192]{1,0:T(8,128)} async-done(((f32[64,1024]{1,0:T(8,128)}), f32[64,8192]{1,0:T(8,128)}) %all-gather.3.cloned.1.call-update) | async-done | bytes 2097168 | tf_op jit(solution)/shard_map/all_gather | solution.py:20
  125.2 4.6 reshape.34
  129.9 6.6 copy.15
  136.5 23.7 %gather_fusion = f32[576,64,64]{2,1,0:T(8,128)} fusion(f32[64,128,64]{2,0,1:T(8,128)} %copy.15, s32[1024]{0:T(1024)S(1)} %pad_clamp_fusion), kind=kCustom, calls=%fused_computation | custom fusion | bytes 18876672 | tf_op jit(solution)/shard_map/gather | solution.py:21
  160.1 26.8 %fusion.2 = f32[576,64,64]{2,1,0:T(8,128)} fusion(f32[64,576,64]{0,2,1:T(8,128)} %bitcast.83, f32[576,64,64]{2,1,0:T(8,128)} %gather_fusion), kind=kOutput, calls=%fused_computation.4 | convolution fusion | flops 1811939328 | bytes 28311552 | tf_op jit(solution)/shard_map/mte,ate->mta/dot_general | solution.py:23
  186.9 17.4 %copy.18 = f32[576,64,64]{0,2,1:T(8,128)} copy(f32[576,64,64]{2,1,0:T(8,128)} %fusion.2) | data formatting | bytes 18874368 | tf_op jit(solution)/shard_map/mte,ate->mta/dot_general | solution.py:23
  204.3 20.0 %fusion.8 = f32[64,48,64]{2,1,0:T(8,128)S(1)} fusion(f32[576,64,64]{0,2,1:T(8,128)} %copy.18, f32[576]{0:T(1024)S(1)} %fusion.68, s32[576]{0:T(1024)S(1)} %copy-done.6), kind=kOutput, calls=%fused_computation.10 | convolution fusion | flops 1359009792 | bytes 10228224 | tf_op jit(solution)/shard_map/fnx,nj->fjx/dot_general | solution.py:29
  224.4 0.4 reshape.36
  224.9 7.3 %collective-permute-start = (f32[64,1024]{1,0:T(8,128)S(1)}, f32[64,1024]{1,0:T(8,128)S(1)}, u32[]{:S(2)}, u32[]{:S(2)}) collective-permute-start(f32[64,1024]{1,0:T(8,128)S(1)} %get-tuple-element.11), channel_id=1, source_target_pairs={{0,8},{8,16},{16,24},{24,32},{32,40},{40,48},{48,56},{56,64},{64,7... | collective-permute-start | bytes 786440 | tf_op jit(solution)/shard_map/ppermute | solution.py:12
  232.2 1.9 collective-permute-start.1
  234.2 1.6 fusion.33
  235.8 4.1 collective-permute-done.1
  239.9 0.1 fusion.37
  240.0 1.7 fusion.18
  241.7 0.4 fusion.88
  242.0 77.3 %psum.43 = f32[64,64]{1,0:T(8,128)S(1)} all-reduce(f32[64,64]{1,0:T(8,128)S(1)} %fusion.88), channel_id=1, replica_groups=mesh['row'=32,'col'=8] {'row','col'}, use_global_device_ids=true, to_apply=%region_1.0 | all-reduce | flops 4096 | bytes 32768 | tf_op jit(solution)/shard_map/psum | solution.py:57
  319.3 1.1 fusion.14
  320.5 2.7 fusion.32
  323.3 1.4 convolution_bitcast_fusion.5
  324.7 2.8 fusion.17
  327.5 2.1 convolution_bitcast_fusion.2
  329.6 2.1 convolution_bitcast_fusion.3
  331.7 22.2 %all-gather.5.cloned.1.call-done = f32[64,8192]{1,0:T(8,128)} async-done(((f32[64,1024]{1,0:T(8,128)}), f32[64,8192]{1,0:T(8,128)}) %all-gather.5.cloned.1.call-update) | async-done | bytes 2097168 | tf_op jit(solution)/shard_map/all_gather | solution.py:20
  353.8 4.8 reshape.37
  358.6 6.6 copy.16
  365.2 23.7 %gather_fusion.1 = f32[576,64,64]{2,1,0:T(8,128)} fusion(f32[64,128,64]{2,0,1:T(8,128)} %copy.16, s32[1024]{0:T(1024)S(1)} %pad_clamp_fusion), kind=kCustom, calls=%fused_computation.1 | custom fusion | bytes 18876672 | tf_op jit(solution)/shard_map/gather | solution.py:21
  388.9 26.6 %fusion = f32[576,64,64]{2,1,0:T(8,128)} fusion(f32[64,576,64]{0,2,1:T(8,128)} %bitcast.84, f32[576,64,64]{2,1,0:T(8,128)} %gather_fusion.1), kind=kOutput, calls=%fused_computation.2 | convolution fusion | flops 1811939328 | bytes 28311552 | tf_op jit(solution)/shard_map/mte,ate->mta/dot_general | solution.py:23
  415.5 17.4 %copy.19 = f32[576,64,64]{0,2,1:T(8,128)} copy(f32[576,64,64]{2,1,0:T(8,128)} %fusion) | data formatting | bytes 18874368 | tf_op jit(solution)/shard_map/mte,ate->mta/dot_general | solution.py:23
  432.9 20.3 %fusion.11 = f32[64,48,64]{2,1,0:T(8,128)S(1)} fusion(f32[576,64,64]{0,2,1:T(8,128)} %copy.19, f32[576]{0:T(1024)S(1)} %fusion.68, s32[576]{0:T(1024)S(1)} %copy-done.6), kind=kOutput, calls=%fused_computation.11 | convolution fusion | flops 1359009792 | bytes 10228224 | tf_op jit(solution)/shard_map/fnx,nj->fjx/dot_general | solution.py:29
  453.1 0.4 reshape.38
  453.6 7.4 %collective-permute-start.2 = (f32[64,1024]{1,0:T(8,128)S(1)}, f32[64,1024]{1,0:T(8,128)S(1)}, u32[]{:S(2)}, u32[]{:S(2)}) collective-permute-start(f32[64,1024]{1,0:T(8,128)S(1)} %get-tuple-element.9), channel_id=1, source_target_pairs={{0,8},{8,16},{16,24},{24,32},{32,40},{40,48},{48,56},{56,64},{64,7... | collective-permute-start | bytes 786440 | tf_op jit(solution)/shard_map/ppermute | solution.py:12
  461.0 1.9 collective-permute-start.3
  463.0 2.5 fusion.31
  465.5 2.3 convolution_bitcast_fusion.4
  467.8 0.9 collective-permute-done.3
  468.7 0.1 fusion.35
  468.8 2.5 fusion.16
  471.3 2.1 convolution_bitcast_fusion
  473.4 2.3 convolution_bitcast_fusion.1
  475.7 249.0 %all-reduce.3.cloned.1.call-done = (f32[192,192]{1,0:T(8,128)}, f32[192,192]{1,0:T(8,128)}, f32[192,192]{1,0:T(8,128)}, f32[192,192]{1,0:T(8,128)}) async-done(((f32[192,192]{1,0:T(8,128)}, f32[192,192]{1,0:T(8,128)}, f32[192,192]{1,0:T(8,128)}, f32[192,192]{1,0:T(8,128)}), (f32[192,192]{1,0:T(8,128)}, f32[192,192]{1,0:T(8,128)}, f32[192,192]{1,0:T(8,128)}, ...) | async-done | bytes 589840 | tf_op jit(solution)/shard_map/psum | solution.py:69
  724.7 1.0 multiply_bitcast_fusion.2
  725.8 1.1 multiply_bitcast_fusion
  726.9 0.9 pad_maximum_fusion.4
  (30 shorter events, 0.3 us)
Async XLA Ops:
  7.2 99.7 %copy-start.7 = (s32[576]{0:T(1024)S(1)}, s32[576]{0:T(1024)}, u32[]{:S(2)}) copy-start(s32[576]{0:T(1024)} %param.17) | copy-start | bytes 6916
  7.2 118.1 %all-gather.3.cloned.1.call-start = ((), (), s32[]{:S(2)}) async-start(), calls=%async_computation | async-start | bytes 2359296 | tf_op jit(solution)/shard_map/all_gather | solution.py:20
  92.4 261.4 %all-gather.5.cloned.1.call-start = ((), (), s32[]{:S(2)}) async-start(), calls=%async_computation.1 | async-start | bytes 2359296 | tf_op jit(solution)/shard_map/all_gather | solution.py:20
  186.9 17.4 %copy-start.6 = (s32[576]{0:T(1024)S(1)}, s32[576]{0:T(1024)}, u32[]{:S(2)}) copy-start(s32[576]{0:T(1024)} %param.16) | copy-start | bytes 6916
  186.9 47.3 %copy-start = (f32[64,1024]{1,0:T(8,128)S(1)}, f32[64,1024]{1,0:T(8,128)}, u32[]{:S(2)}) copy-start(f32[64,1024]{1,0:T(8,128)} %fusion.15) | copy-start | bytes 786436
  186.9 47.3 %copy-start.4 = (f32[64,1024]{1,0:T(8,128)S(1)}, f32[64,1024]{1,0:T(8,128)}, u32[]{:S(2)}) copy-start(f32[64,1024]{1,0:T(8,128)} %param.10) | copy-start | bytes 786436
  186.9 47.3 %copy-start.5 = (f32[2,192,64]{1,2,0:T(8,128)S(1)}, f32[2,192,64]{1,2,0:T(8,128)}, u32[]{:S(2)}) copy-start(f32[2,192,64]{1,2,0:T(8,128)} %param.19) | copy-start | bytes 294916
  186.9 53.0 %copy-start.2 = (f32[64,1024]{1,0:T(8,128)S(1)}, f32[64,1024]{1,0:T(8,128)}, u32[]{:S(2)}) copy-start(f32[64,1024]{1,0:T(8,128)} %param.14) | copy-start | bytes 786436
  224.9 10.9 %collective-permute-start = (f32[64,1024]{1,0:T(8,128)S(1)}, f32[64,1024]{1,0:T(8,128)S(1)}, u32[]{:S(2)}, u32[]{:S(2)}) collective-permute-start(f32[64,1024]{1,0:T(8,128)S(1)} %get-tuple-element.11), channel_id=1, source_target_pairs={{0,8},{8,16},{16,24},{24,32},{32,40},{40,48},{48,56},{56,64},{64,7... | collective-permute-start | bytes 786440 | tf_op jit(solution)/shard_map/ppermute | solution.py:12
  232.2 7.7 %collective-permute-start.1 = (f32[64,1024]{1,0:T(8,128)S(1)}, f32[64,1024]{1,0:T(8,128)S(1)}, u32[]{:S(2)}, u32[]{:S(2)}) collective-permute-start(f32[64,1024]{1,0:T(8,128)S(1)} %get-tuple-element.12), channel_id=1, source_target_pairs={{8,0},{16,8},{24,16},{32,24},{40,32},{48,40},{56,48},{64,56},{72,6... | collective-permute-start | bytes 786440 | tf_op jit(solution)/shard_map/ppermute | solution.py:12
  320.5 404.2 %all-reduce.3.cloned.1.call-start = ((), (), s32[]{:S(2)}) async-start(), calls=%async_computation.2 | async-start | bytes 1572864 | tf_op jit(solution)/shard_map/psum | solution.py:69
  324.7 64.2 %copy-start.3 = (f32[64,1024]{1,0:T(8,128)}, f32[64,1024]{1,0:T(8,128)S(1)}, u32[]{:S(2)}) copy-start(f32[64,1024]{1,0:T(8,128)S(1)} %convolution_bitcast_fusion.5) | copy-start | bytes 786436
  415.5 47.4 %copy-start.1 = (f32[64,1024]{1,0:T(8,128)S(1)}, f32[64,1024]{1,0:T(8,128)}, u32[]{:S(2)}) copy-start(f32[64,1024]{1,0:T(8,128)} %fusion.14) | copy-start | bytes 786436
  453.6 14.1 %collective-permute-start.2 = (f32[64,1024]{1,0:T(8,128)S(1)}, f32[64,1024]{1,0:T(8,128)S(1)}, u32[]{:S(2)}, u32[]{:S(2)}) collective-permute-start(f32[64,1024]{1,0:T(8,128)S(1)} %get-tuple-element.9), channel_id=1, source_target_pairs={{0,8},{8,16},{16,24},{24,32},{32,40},{40,48},{48,56},{56,64},{64,7... | collective-permute-start | bytes 786440 | tf_op jit(solution)/shard_map/ppermute | solution.py:12
  461.0 7.7 %collective-permute-start.3 = (f32[64,1024]{1,0:T(8,128)S(1)}, f32[64,1024]{1,0:T(8,128)S(1)}, u32[]{:S(2)}, u32[]{:S(2)}) collective-permute-start(f32[64,1024]{1,0:T(8,128)S(1)} %get-tuple-element.10), channel_id=1, source_target_pairs={{8,0},{16,8},{24,16},{32,24},{40,32},{48,40},{56,48},{64,56},{72,6... | collective-permute-start | bytes 786440 | tf_op jit(solution)/shard_map/ppermute | solution.py:12
Sparse Core Ops, SparseCore 0:
  92.5 32.6 all-gather.2
  320.6 33.1 all-gather.4
  471.5 253.1 all-reduce.2
where the time goes:
time: 746 us; the launch traced here: 735 us
  waiting for transfers between devices  295 us (40%)
  blocking collectives  159 us (21%)
  matrix products  125 us (17%)
  local copies, waits for them, and re-layouts  120 us (16%)
  starting transfers between devices  18.7 us (3%)
  between operations  15.1 us (2%)
    psum x1, waiting for transfers between devices, body(): gram_a, gram_b = lax.psum((local_a, local_b), ('row', 'col'))  249 us
    psum x2, blocking collectives, body(): rayleigh_block = lax.psum(local_block, ('row', 'col')) / total  159 us
    dot_general x2, matrix products, apply_stiffness(): jnp.einsum('mte,ate->mta', picked, slabs, precision=PRECISION_TOP)  53.4 us
    gather x2, local copies, waits for them, and re-layouts, apply_stiffness(): picked = gathered.reshape(modes, -1, width)[:, tile_cols, :]  47.3 us
    all_gather x2, waiting for transfers between devices, apply_stiffness(): gathered = lax.all_gather(field, 'col', axis=1, tiled=True)  40.5 us
    dot_general x2, matrix products, apply_stiffness(): jnp.einsum('fnx,nj->fjx', matrix_product, select_entries, precision=PRECI...  40.3 us
    dot_general x2, local copies, waits for them, and re-layouts, apply_stiffness(): jnp.einsum('mte,ate->mta', picked, slabs, precision=PRECISION_TOP)  34.8 us
    reshape x4, local copies, waits for them, and re-layouts, apply_stiffness(): picked = gathered.reshape(modes, -1, width)[:, tile_cols, :]  22.6 us
  transfers between devices with their start and end apart: 7, of which 5 were waited for; matrix products, arithmetic and copies ran while one was open for 5% of the time, Pallas kernels for 0%

commit v1 on v0

v1 whole, which is shorter than its diff:
```python
import functools

import jax
import jax.numpy as jnp
from jax import lax
from jax.experimental import pallas as pl
from jax.experimental.pallas import tpu as pltpu
from jax.sharding import PartitionSpec as P

F32 = jnp.float32
BF16 = jnp.bfloat16
MESH = pl.DeviceIdType.MESH
DMA = pltpu.SemaphoreType.DMA

MODES, TILE, BPD, SLOTS = 64, 64, 16, 576
NROW, NCOL = 32, 8
LOCAL = TILE * BPD
DOFS = LOCAL * NROW * NCOL
PLANE, DEEP = 8, 4
SIZES = {"xc": PLANE, "y": DEEP, "z": NCOL}
LANES = 128
STRIPS = LOCAL // LANES
BLOCKS = NCOL * BPD
WIDE = BLOCKS * TILE
PARTS = 4
HOPS = 3 * PARTS + PARTS // 2
CHUNKS, PAIRS = 4, 12


def halves(value):
    high = value.astype(BF16)
    return high, (value - high.astype(F32)).astype(BF16)


def product(a, b, dims):
    dot = functools.partial(
        lax.dot_general, dimension_numbers=(dims, ((), ())), preferred_element_type=F32
    )
    a_high, a_low = halves(a)
    b_high, b_low = halves(b)
    return dot(a_high, b_high) + (dot(a_high, b_low) + dot(a_low, b_high))


NN = ((1,), (0,))
NT = ((1,), (1,))
TN = ((0,), (0,))


class Place:
    def __init__(self):
        i, j = lax.axis_index("row"), lax.axis_index("col")
        self.i, self.j = i, j
        plane, inner = i // PLANE, lax.rem(i, PLANE)
        self.groups = {
            "xc": (PLANE, inner, lambda m: (plane * PLANE + m, j)),
            "y": (DEEP, plane, lambda m: (m * PLANE + inner, j)),
            "z": (NCOL, j, lambda m: (i, m)),
        }
        self.next_row = (lax.rem(i + 1, NROW), j)
        self.last_row = (lax.rem(i + NROW - 1, NROW), j)
        self.right = (i, lax.rem(j + 1, NCOL))
        self.left = (i, lax.rem(j + NCOL - 1, NCOL))


def greet(place, rows):
    barrier = pltpu.get_barrier_semaphore()
    devices = [place.next_row, place.last_row] if rows else []
    for size, me, device in place.groups.values():
        devices += [device(lax.rem(me + o, size)) for o in range(1, size)]
    for device in devices:
        pl.semaphore_signal(barrier, inc=1, device_id=device, device_id_type=MESH)
    return lambda: pl.semaphore_wait(barrier, len(devices))


def swap(place, name, source, landing, sends, recvs):
    size, me, device = place.groups[name]
    copies = []
    for o in range(1, size):
        peer = lax.rem(me + o, size)
        copy = pltpu.make_async_remote_copy(
            src_ref=source(peer),
            dst_ref=landing.at[me],
            send_sem=sends.at[o],
            recv_sem=recvs.at[o],
            device_id=device(peer),
            device_id_type=MESH,
        )
        copy.start()
        copies.append(copy)
    return copies


def finish(copies):
    for copy in copies:
        copy.wait()


def total(landing):
    value = landing[0]
    for m in range(1, landing.shape[0]):
        value = value + landing[m]
    return value


def theta_scratch():
    shapes = [pltpu.VMEM((SIZES[n], 32, LANES), F32) for n in SIZES]
    return shapes + [DMA((SIZES[n],)) for n in SIZES for _ in range(2)]


def sum_theta(place, local, scratch):
    value = jnp.concatenate([local[:32], local[32:]], axis=1)
    for at, name in enumerate(SIZES):
        landing, sends, recvs = scratch[at], scratch[3 + 2 * at], scratch[4 + 2 * at]
        me = place.groups[name][1]
        landing[me] = value
        finish(swap(place, name, lambda peer: landing.at[me], landing, sends, recvs))
        value = total(landing)
    return jnp.concatenate([value[:, :64], value[:, 64:]], axis=0)


STAGES = ("xc", "y", "z", "y", "xc")


def mix_scratch(rows):
    r = rows // NROW
    big, mid = (PLANE, DEEP, r, LANES), (DEEP, r, LANES)
    shapes = [big, big, mid, mid, (NCOL, r, LANES), mid, big]
    return [pltpu.VMEM(s, F32) for s in shapes] + [
        DMA((SIZES[n],)) for n in STAGES for _ in range(2)
    ]


def mix(place, rows, flat, scratch):
    r = rows // NROW
    data, land_a, half, land_b, land_z, back, result = scratch[:7]
    sems = [scratch[7 + 2 * n : 9 + 2 * n] for n in range(5)]
    mine = {name: place.groups[name][1] for name in SIZES}
    for a in range(PLANE):
        for b in range(DEEP):
            at = (a * DEEP + b) * r
            data[a, b] = flat[at : at + r, :]
    land_a[mine["xc"]] = data[mine["xc"]]
    copies = swap(place, "xc", lambda peer: data.at[peer], land_a, *sems[0])
    yield
    finish(copies)
    half[...] = total(land_a)
    land_b[mine["y"]] = half[mine["y"]]
    copies = swap(place, "y", lambda peer: half.at[peer], land_b, *sems[1])
    yield
    finish(copies)
    land_z[mine["z"]] = total(land_b)
    copies = swap(place, "z", lambda peer: land_z.at[mine["z"]], land_z, *sems[2])
    yield
    finish(copies)
    back[mine["y"]] = total(land_z)
    copies = swap(place, "y", lambda peer: back.at[mine["y"]], back, *sems[3])
    yield
    finish(copies)
    result[mine["xc"]] = back[...]
    copies = swap(place, "xc", lambda peer: result.at[mine["xc"]], result, *sems[4])
    yield
    finish(copies)


def unmix(rows, result, flat):
    r = rows // NROW
    for a in range(PLANE):
        for b in range(DEEP):
            at = (a * DEEP + b) * r
            flat[at : at + r, :] = result[a, b]


def ring_scratch():
    return [
        pltpu.VMEM((NCOL, STRIPS, MODES, LANES), F32),
        DMA((2, HOPS)),
        DMA((2, HOPS)),
    ]


def ring(place, scratch, spread_ref, beside=None):
    held, sends, recvs = scratch
    per = STRIPS // PARTS
    devices = (place.right, place.left)

    def region(way, n, hop):
        q, s = n // PARTS, lax.rem(n, PARTS)
        if way == 0:
            return lax.rem(place.j + 2 * NCOL - q - hop, NCOL), s
        return lax.rem(place.j + q + hop, NCOL), PARTS - 1 - s

    def copy(way, n, hop=0):
        slot, part = region(way, n, hop)
        piece = held.at[slot, pl.ds(part * per, per)]
        return pltpu.make_async_remote_copy(
            src_ref=piece,
            dst_ref=piece,
            send_sem=sends.at[way, n],
            recv_sem=recvs.at[way, n],
            device_id=devices[way],
            device_id_type=MESH,
        )

    def spread(slot, first, count):
        def one(b, carry):
            value = held[slot, first + b]
            high = value.astype(BF16).astype(F32)
            at = pl.multiple_of((slot * STRIPS + first + b) * LANES, LANES)
            both = jnp.concatenate([high, value - high], axis=0)
            spread_ref[pl.ds(at, LANES), :] = both.T.astype(BF16)
            return carry

        lax.fori_loop(0, count, one, 0)

    def begin(n, carry):
        for way in range(2):
            copy(way, n).start()
        return carry

    def step(n, carry):
        for way in range(2):
            copy(way, n, 1).wait_recv()

            @pl.when(n + PARTS < HOPS)
            def forward():
                copy(way, n + PARTS).start()

        for way in range(2):
            slot, part = region(way, n, 1)
            spread(slot, part * per, per)
        return carry

    def end(n, carry):
        for way in range(2):
            copy(way, n).wait_send()
        return carry

    lax.fori_loop(0, PARTS, begin, 0)
    if beside is not None:
        next(beside)
    spread_ref[WIDE : WIDE + TILE, :] = jnp.zeros((TILE, LANES), BF16)
    spread(place.j, 0, STRIPS)
    stops = (0, 4, 6, 8, 10, HOPS) if beside is not None else (0, HOPS)
    for a, b in zip(stops[:-1], stops[1:]):
        lax.fori_loop(a, b, step, 0)
        if beside is not None:
            next(beside, None)
    if beside is not None:
        for _ in beside:
            pass
    lax.fori_loop(0, HOPS, end, 0)


def correct(place, x_ref, ax_ref, diag_ref, theta_t, w_ref, held):
    for s in range(STRIPS):
        at = slice(s * LANES, (s + 1) * LANES)
        residual = ax_ref[:, at] - product(theta_t, x_ref[:, at], NN)
        w = residual / diag_ref[:, at]
        w_ref[:, at] = w
        held[place.j, s] = w


def theta_local(x_ref, ax_ref):
    return product(ax_ref[...], x_ref[...], NT) * (1.0 / DOFS)


def fold(value):
    return jnp.concatenate([value[:96], value[96:]], axis=1)


def gram_rest(x_ref, w_ref, p_ref, ax_ref, ap_ref, flat, base):
    basis = jnp.concatenate([x_ref[...], w_ref[...], p_ref[...]], axis=0)
    other = jnp.concatenate([ax_ref[...], ap_ref[...], basis], axis=0)
    block = product(basis, other, NT) * (1.0 / DOFS)
    flat[base : base + 192, :] = block[:, :128]
    flat[base + 192 : base + 384, :] = block[:, 128:256]
    flat[base + 384 : base + 480, :] = fold(block[:, 256:])


def gram_image(x_ref, w_ref, p_ref, aw_ref, flat):
    basis = jnp.concatenate([x_ref[...], w_ref[...], p_ref[...]], axis=0)
    flat[0:96, :] = fold(product(basis, aw_ref[...], NT) * (1.0 / DOFS))


def halo_scratch():
    return [pltpu.VMEM((MODES, LOCAL), F32)] * 2 + [DMA((2,)), DMA((2,))]


def halo(place, part_ref, scratch):
    above, below, sends, recvs = scratch
    copies = []
    for at, (first, landing, device) in enumerate(
        ((0, above, place.last_row), (2 * LOCAL, below, place.next_row))
    ):
        copy = pltpu.make_async_remote_copy(
            src_ref=part_ref.at[:, pl.ds(first, LOCAL)],
            dst_ref=landing,
            send_sem=sends.at[at],
            recv_sem=recvs.at[at],
            device_id=device,
            device_id_type=MESH,
        )
        copy.start()
        copies.append(copy)
    return copies


def image(part_ref, w_ref, diag_ref, above, below, aw_ref):
    aw_ref[...] = (
        part_ref[:, LOCAL : 2 * LOCAL]
        + below[...]
        + above[...]
        + diag_ref[...] * w_ref[...]
    )


def rotate(turn, x, w, p, next_x, next_p):
    moved = product(turn[64:], jnp.concatenate([w[...], p[...]], axis=0), TN)
    next_p[...] = moved
    next_x[...] = product(turn[:64], x[...], TN) + moved


def opening(x, p, ax, ap, diag, w, spread_ref, sums, *scratch):
    place = Place()
    ready = greet(place, rows=False)
    theta = scratch[:9]
    ring_set = scratch[9:12]
    flat = scratch[12]
    mixing = scratch[13:]
    local = theta_local(x, ax)
    ready()
    theta_t = sum_theta(place, local, theta)
    correct(place, x, ax, diag, theta_t, w, ring_set[0])

    def beside():
        gram_rest(x, w, p, ax, ap, flat, 0)
        yield from mix(place, 480, flat, mixing)
        sums[...] = mixing[6][...]

    ring(place, ring_set, spread_ref, beside())


def middle(
    part, turn, x, w, p, ax, ap, diag,
    x1, w1, p1, ax1, ap1, spread_ref, sums, *scratch,
):
    place = Place()
    ready = greet(place, rows=True)
    theta = scratch[:9]
    ring_set = scratch[9:12]
    flat, aw = scratch[12:14]
    around = scratch[14:18]
    mixing = scratch[18:]
    ready()
    copies = halo(place, part, around)
    rotate(turn[0], x, w, p, x1, p1)
    finish(copies)
    image(part, w, diag, around[0], around[1], aw)
    rotate(turn[0], ax, aw, ap, ax1, ap1)
    theta_t = sum_theta(place, theta_local(x1, ax1), theta)
    correct(place, x1, ax1, diag, theta_t, w1, ring_set[0])

    def beside():
        gram_image(x, w, p, aw, flat)
        gram_rest(x1, w1, p1, ax1, ap1, flat, 96)
        yield from mix(place, 576, flat, mixing)
        sums[...] = mixing[6][...]

    ring(place, ring_set, spread_ref, beside())


def put_grams(rest, image_block, grams, k):
    left = jnp.concatenate([image_block[:, :64], image_block[:, 64:]], axis=0)
    block = rest[0:192]
    grams[k, 0] = jnp.concatenate([block[:, :64], left, block[:, 64:]], axis=1)
    tail = rest[384:480]
    grams[k, 1] = jnp.concatenate(
        [rest[192:384], jnp.concatenate([tail[:, :64], tail[:, 64:]], axis=0)], axis=1
    )


def closing(
    part, turn, x, w, p, ax, ap, diag, sums0, sums1,
    x2, p2, ax2, ap2, grams, *scratch,
):
    place = Place()
    ready = greet(place, rows=True)
    flat, aw, flat0, flat1 = scratch[:4]
    around = scratch[4:8]
    mixing = scratch[8:]
    ready()
    copies = halo(place, part, around)
    unmix(480, sums0, flat0)
    unmix(576, sums1, flat1)
    put_grams(flat0[...], flat1[0:96], grams, 0)
    rotate(turn[1], x, w, p, x2, p2)
    finish(copies)
    image(part, w, diag, around[0], around[1], aw)
    gram_image(x, w, p, aw, flat)
    steps = mix(place, 96, flat, mixing)
    next(steps)
    rotate(turn[1], ax, aw, ap, ax2, ap2)
    for _ in steps:
        pass
    unmix(96, mixing[6], flat)
    put_grams(flat1[96:576], flat[0:96], grams, 1)


def sparse(cols, rows, count, tiles, spread_ref, part, total_ref):
    step = pl.program_id(0)
    pairs = SLOTS // 2 // CHUNKS

    @pl.when(step == 0)
    def clear():
        total_ref[...] = jnp.zeros_like(total_ref)

    live = count[0]
    left = jnp.clip((live - step * pairs * 2 + 1) // 2, 0, pairs)
    nothing = jnp.zeros((TILE, LANES), BF16)

    def block(slot):
        column = jnp.where(slot < live, cols[slot], BLOCKS)
        return spread_ref[pl.ds(pl.multiple_of(column * TILE, TILE), TILE), :]

    def some(s, carry):
        found = []
        for u in range(PAIRS):
            q = s * PAIRS + u
            slot = (step * pairs + q) * 2
            high, low = halves(tiles[:, pl.ds(pl.multiple_of(q * LANES, LANES), LANES)])
            table = jnp.concatenate(
                [
                    jnp.concatenate([block(slot), nothing], axis=1),
                    jnp.concatenate([nothing, block(slot + 1)], axis=1),
                ],
                axis=0,
            )
            out = jnp.dot(
                jnp.concatenate([high, low], axis=0), table, preferred_element_type=F32
            )
            out = out[:TILE] + out[TILE:]
            found.append((rows[slot], out[:, :LANES]))
            found.append((rows[slot + 1], out[:, LANES:]))
        for row, value in found:
            total_ref[row] += value
        return carry

    lax.fori_loop(0, (left + PAIRS - 1) // PAIRS, some, 0)

    @pl.when(step == CHUNKS - 1)
    def write():
        def one(b, carry):
            both = jnp.concatenate([total_ref[2 * b], total_ref[2 * b + 1]], axis=0).T
            at = pl.multiple_of(b * LANES, LANES)
            part[:, pl.ds(at, LANES)] = both[:MODES] + both[MODES:]
            return carry

        lax.fori_loop(0, 3 * BPD // 2, one, 0, unroll=4)


FIELD = jax.ShapeDtypeStruct((MODES, LOCAL), F32)
SPREAD = jax.ShapeDtypeStruct((WIDE + TILE, LANES), BF16)


def talking(kernel, outs, scratch, number):
    whole = pl.BlockSpec(memory_space=pltpu.VMEM)
    return lambda *args: pl.pallas_call(
        kernel,
        out_shape=outs,
        in_specs=[whole] * len(args),
        out_specs=[whole] * len(outs),
        scratch_shapes=scratch,
        compiler_params=pltpu.CompilerParams(
            collective_id=number, has_side_effects=True, vmem_limit_bytes=48 << 20
        ),
        name=kernel.__name__,
    )(*args)


def sparse_product(cols, rows, count, tiles, spread_value):
    return pl.pallas_call(
        sparse,
        grid_spec=pltpu.PrefetchScalarGridSpec(
            num_scalar_prefetch=3,
            grid=(CHUNKS,),
            in_specs=[
                pl.BlockSpec((TILE, SLOTS * TILE // CHUNKS), lambda g, *_: (0, g)),
                pl.BlockSpec((WIDE + TILE, LANES), lambda g, *_: (0, 0)),
            ],
            out_specs=pl.BlockSpec((MODES, 3 * LOCAL), lambda g, *_: (0, 0)),
            scratch_shapes=[pltpu.VMEM((3 * BPD, TILE, LANES), F32)],
        ),
        out_shape=jax.ShapeDtypeStruct((MODES, 3 * LOCAL), F32),
        compiler_params=pltpu.CompilerParams(vmem_limit_bytes=48 << 20),
        name="sparse",
    )(cols, rows, count, tiles, spread_value)


def sums_of(rows):
    return jax.ShapeDtypeStruct((PLANE, DEEP, rows // NROW, LANES), F32)


def flat_of(rows):
    return pltpu.VMEM((rows, LANES), F32)


def body(x, p, ax, ap, diag, tiles, rows, cols, count, turns):
    field = pltpu.VMEM((MODES, LOCAL), F32)
    w, spread0, sums0 = talking(
        opening,
        [FIELD, SPREAD, sums_of(480)],
        theta_scratch() + ring_scratch() + [flat_of(480)] + mix_scratch(480),
        1,
    )(x, p, ax, ap, diag)
    part = sparse_product(cols, rows, count, tiles, spread0)
    x1, w1, p1, ax1, ap1, spread1, sums1 = talking(
        middle,
        [FIELD] * 5 + [SPREAD, sums_of(576)],
        theta_scratch()
        + ring_scratch()
        + [flat_of(576), field]
        + halo_scratch()
        + mix_scratch(576),
        2,
    )(part, turns, x, w, p, ax, ap, diag)
    part1 = sparse_product(cols, rows, count, tiles, spread1)
    return talking(
        closing,
        [FIELD] * 4 + [jax.ShapeDtypeStruct((2, 2, 192, 192), F32)],
        [flat_of(96), field, flat_of(480), flat_of(576)]
        + halo_scratch()
        + mix_scratch(96),
        3,
    )(part1, turns, x1, w1, p1, ax1, ap1, diag, sums0, sums1)


def solution(mesh):
    split = P(None, ("row", "col"))
    listed = P(("row", "col"))
    return jax.shard_map(
        lambda *args: tuple(body(*args)),
        mesh=mesh,
        in_specs=(split,) * 6 + (listed,) * 3 + (P(),),
        out_specs=(split,) * 4 + (P(),),
        check_vma=False,
    )
```

time: 746 us -> 173 us (0.23); the launches traced: 735 us -> 173 us
  waiting for transfers between devices: 295 us -> 0 us
  Pallas kernels: 0 us -> 159 us
  blocking collectives: 159 us -> 0 us
  matrix products: 125 us -> 0 us
  local copies, waits for them, and re-layouts: 120 us -> 12.4 us
  starting transfers between devices: 18.7 us -> 0 us
  between operations: 15.1 us -> 1.4 us
    psum x1 -> x0, waiting for transfers between devices: 249 us -> none  [body(): gram_a, gram_b = lax.psum((local_a, local_b), ('row', 'col'))]
    pallas_call x0 -> x5, Pallas kernels: none -> 159 us  [the longest x3 143 us: talking(): pl.pallas_call(kernel, out_shape=outs, in_specs=[whole] * len(args), out_...]
    psum x2 -> x0, blocking collectives: 159 us -> none  [body(): rayleigh_block = lax.psum(local_block, ('row', 'col')) / total]
    dot_general x20 -> x0, matrix products: 125 us -> none  [the longest x2 53.4 us: apply_stiffness(): jnp.einsum('mte,ate->mta', picked, slabs, precision=PRECISION_TOP)]
    gather x2 -> x0, local copies, waits for them, and re-layouts: 47.3 us -> none  [apply_stiffness(): picked = gathered.reshape(modes, -1, width)[:, tile_cols, :]]
    all_gather x2 -> x0, waiting for transfers between devices: 40.5 us -> none  [apply_stiffness(): gathered = lax.all_gather(field, 'col', axis=1, tiled=True)]
    reshape x7 -> x0, local copies, waits for them, and re-layouts: 37.3 us -> none  [the longest x4 22.6 us: apply_stiffness(): picked = gathered.reshape(modes, -1, width)[:, tile_cols, :]]
    dot_general x2 -> x0, local copies, waits for them, and re-layouts: 34.8 us -> none  [apply_stiffness(): jnp.einsum('mte,ate->mta', picked, slabs, precision=PRECISION_TOP)]
  transfers between devices with their start and end apart: 7 -> 0, of which waited for: 5 -> 0; matrix products, arithmetic and copies ran while one was open for 5% -> 0% of each run, Pallas kernels for 0% -> 0%
where the time goes in v1:
time: 173 us
  Pallas kernels  159 us (92%)
  local copies, waits for them, and re-layouts  12.4 us (7%)
    pallas_call x3, Pallas kernels, talking(): pl.pallas_call(kernel, out_shape=outs, in_specs=[whole] * len(args), out_...  143 us
    pallas_call x2, Pallas kernels, sparse_product(): pl.pallas_call(sparse, grid_spec=pltpu.PrefetchScalarGridSpec(num_scalar_...  16.3 us
    unnamed x28, local copies, waits for them, and re-layouts  12.4 us

profile of v1, /device:TPU:1, one launch (start us, length us, event | category | flops | bytes accessed | tf_op | source)
XLA Modules:
  0.0 172.8 jit_solution(15162508008176362974)
XLA Ops:
  1.3 1.0 copy.15.turn
  2.3 0.0 copy-start
  2.3 0.9 copy-done
  3.3 0.0 copy-start.3
  3.3 0.9 copy-done.3
  4.2 0.0 copy-start.4
  4.2 0.9 copy-done.4
  5.2 0.0 copy-start.5
  5.2 0.9 copy-done.5
  6.1 0.0 copy-start.6
  6.1 0.9 copy-done.6
  7.1 51.9 %opening.1 = (f32[64,1024]{1,0:T(8,128)S(1)}, bf16[8256,128]{1,0:T(8,128)(2,1)S(1)}, f32[8,4,15,128]{3,2,1,0:T(8,128)S(1)}) custom-call(f32[64,1024]{1,0:T(8,128)S(1)} %copy-done.3, f32[64,1024]{1,0:T(8,128)S(1)} %copy-done.4, f32[64,1024]{1,0:T(8,128)S(1)} %copy-done.5, f32[64,1024]{1,0:T(8,128)S(1)} %copy-done.6, f32[64,1024]{1,0:T(8,128)S(1)} %copy-done), custom_call_target="tpu_custom_call" | custom-call | tf_op jit(solution)/shard_map/opening/pallas_call | solution.py:467
  59.0 0.0 copy-start.7
  59.0 0.7 copy-done.7
  59.6 0.0 copy-start.9
  59.6 0.7 copy-done.9
  60.3 0.0 copy-start.1
  60.3 8.2 %sparse.2.part = f32[64,3072]{1,0:T(8,128)S(1)} custom-call(s32[576]{0:T(1024)S(1)} %copy-done.7, s32[576]{0:T(1024)S(1)} %copy-done.9, s32[1]{0:T(128)S(6)} %copy.22.count, f32[64,36864]{1,0:T(8,128)} %tiles.3, bf16[8256,128]{1,0:T(8,128)(2,1)S(1)} %get-tuple-element.15.spread_ref), custom_call_target="tpu_custom_call" | custom-call | tf_op jit(solution)/shard_map/sparse/pallas_call | solution.py:481
  68.5 0.0 copy-done.1
  68.5 0.0 copy-start.8
  68.5 0.0 copy-start.10
  68.5 58.9 %middle.1 = (f32[64,1024]{1,0:T(8,128)S(1)}, f32[64,1024]{1,0:T(8,128)S(1)}, f32[64,1024]{1,0:T(8,128)S(1)}, f32[64,1024]{1,0:T(8,128)S(1)}, f32[64,1024]{1,0:T(...) custom-call(f32[64,3072]{1,0:T(8,128)S(1)} %sparse.2.part, f32[2,192,64]{2,1,0:T(8,128)S(1)} %copy.15.turn, ...), custom_call_target="tpu_custom_call" | custom-call | tf_op jit(solution)/shard_map/middle/pallas_call | solution.py:467
  127.5 0.0 copy-done.8
  127.5 0.0 copy-done.10
  127.5 0.0 copy-start.2
  127.5 1.6 copy-done.2
  129.1 8.2 %sparse.3.part = f32[64,3072]{1,0:T(8,128)S(1)} custom-call(s32[576]{0:T(1024)S(1)} %copy-done.8, s32[576]{0:T(1024)S(1)} %copy-done.10, s32[1]{0:T(128)S(6)} %copy.22.count, f32[64,36864]{1,0:T(8,128)} %tiles.3, bf16[8256,128]{1,0:T(8,128)(2,1)S(1)} %copy-done.2), custom_call_target="tpu_custom_call" | custom-call | tf_op jit(solution)/shard_map/sparse/pallas_call | solution.py:481
  137.3 31.8 %closing.1 = (f32[64,1024]{1,0:T(8,128)S(1)}, f32[64,1024]{1,0:T(8,128)S(1)}, f32[64,1024]{1,0:T(8,128)S(1)}, f32[64,1024]{1,0:T(8,128)S(1)}, f32[2,2,192,192]{3,2,1,0:T(8,128)S(1)}) custom-call(f32[64,3072]{1,0:T(8,128)S(1)} %sparse.3.part, f32[2,192,64]{2,1,0:T(8,128)S(1)} %copy.15.turn, f32[64,1024]{1,0:T(8,128)S(1)} %get-tuple-element.18.x, ...), custom_call_target="tpu_custom_call" | custom-call | tf_op jit(solution)/shard_map/closing/pallas_call | solution.py:467
  169.1 0.7 copy.23
  169.8 0.7 copy.24
  170.5 0.7 copy.25
  171.2 0.7 copy.26
  171.9 0.9 copy.27
Async XLA Ops:
  2.3 1.0 copy-start
  3.3 0.9 copy-start.3
  4.2 0.9 copy-start.4
  5.2 0.9 copy-start.5
  6.1 0.9 copy-start.6
  59.0 0.7 copy-start.7
  59.6 0.7 copy-start.9
  60.3 8.2 %copy-start.1 = (f32[64,1024]{1,0:T(8,128)S(1)}, f32[64,1024]{1,0:T(8,128)}, u32[]{:S(2)}) copy-start(f32[64,1024]{1,0:T(8,128)} %diag.5) | copy-start | bytes 786436
  68.5 59.0 %copy-start.8 = (s32[576]{0:T(1024)S(1)}, s32[576]{0:T(1024)}, u32[]{:S(2)}) copy-start(s32[576]{0:T(1024)} %cols.3) | copy-start | bytes 6916
  68.5 59.0 %copy-start.10 = (s32[576]{0:T(1024)S(1)}, s32[576]{0:T(1024)}, u32[]{:S(2)}) copy-start(s32[576]{0:T(1024)} %rows.3) | copy-start | bytes 6916
  127.5 1.6 copy-start.2

commit v2 on v1

v2 whole, which is shorter than its diff:
```python
import functools

import jax
import jax.numpy as jnp
from jax import lax
from jax.experimental import pallas as pl
from jax.experimental.pallas import tpu as pltpu
from jax.sharding import PartitionSpec as P

F32 = jnp.float32
I32 = jnp.int32
BF16 = jnp.bfloat16
MESH = pl.DeviceIdType.MESH
DMA = pltpu.SemaphoreType.DMA

MODES, TILE, BPD, SLOTS = 64, 64, 16, 576
NROW, NCOL = 32, 8
LOCAL = TILE * BPD
DOFS = LOCAL * NROW * NCOL
PLANE, DEEP = 8, 4
SIZES = {"xc": PLANE, "y": DEEP, "z": NCOL}
LANES = 128
STRIPS = LOCAL // LANES
BLOCKS = NCOL * BPD
ROWS = 3 * BPD
PARTS = 4
HOPS = 3 * PARTS + PARTS // 2
RANKS = 640
PAIRS = SLOTS // 2 + ROWS // 2
BATCH = 24
FRESH = 1 << 18


def halves(value):
    high = value.astype(BF16)
    return high, (value - high.astype(F32)).astype(BF16)


def product(a, b, dims):
    dot = functools.partial(
        lax.dot_general, dimension_numbers=(dims, ((), ())), preferred_element_type=F32
    )
    a_high, a_low = halves(a)
    b_high, b_low = halves(b)
    return dot(a_high, b_high) + (dot(a_high, b_low) + dot(a_low, b_high))


NN = ((1,), (0,))
NT = ((1,), (1,))
TN = ((0,), (0,))


class Place:
    def __init__(self):
        i, j = lax.axis_index("row"), lax.axis_index("col")
        self.i, self.j = i, j
        plane, inner = i // PLANE, lax.rem(i, PLANE)
        self.groups = {
            "xc": (PLANE, inner, lambda m: (plane * PLANE + m, j)),
            "y": (DEEP, plane, lambda m: (m * PLANE + inner, j)),
            "z": (NCOL, j, lambda m: (i, m)),
        }
        self.next_row = (lax.rem(i + 1, NROW), j)
        self.last_row = (lax.rem(i + NROW - 1, NROW), j)
        self.right = (i, lax.rem(j + 1, NCOL))
        self.left = (i, lax.rem(j + NCOL - 1, NCOL))


def greet(place, rows):
    barrier = pltpu.get_barrier_semaphore()
    devices = [place.next_row, place.last_row] if rows else []
    for size, me, device in place.groups.values():
        devices += [device(lax.rem(me + o, size)) for o in range(1, size)]
    for device in devices:
        pl.semaphore_signal(barrier, inc=1, device_id=device, device_id_type=MESH)
    return lambda: pl.semaphore_wait(barrier, len(devices))


def swap(place, name, source, landing, sends, recvs):
    size, me, device = place.groups[name]
    copies = []
    for o in range(1, size):
        peer = lax.rem(me + o, size)
        copy = pltpu.make_async_remote_copy(
            src_ref=source(peer),
            dst_ref=landing.at[me],
            send_sem=sends.at[o],
            recv_sem=recvs.at[o],
            device_id=device(peer),
            device_id_type=MESH,
        )
        copy.start()
        copies.append(copy)
    return copies


def finish(copies):
    for copy in copies:
        copy.wait()


def total(landing):
    value = landing[0]
    for m in range(1, landing.shape[0]):
        value = value + landing[m]
    return value


class Scratch:
    def __init__(self, shapes):
        self.names, self.shapes = list(shapes), list(shapes.values())

    def found(self, refs):
        return dict(zip(self.names, refs))


def sum_theta(place, local, refs, tag, work):
    value = jnp.concatenate([local[:32], local[32:]], axis=1)
    for at, name in enumerate(SIZES):
        landing = refs[f"{tag}_{name}"]
        me = place.groups[name][1]
        landing[me] = value
        copies = swap(
            place,
            name,
            lambda peer: landing.at[me],
            landing,
            refs[f"{tag}_{name}_s"],
            refs[f"{tag}_{name}_r"],
        )
        work[at]()
        finish(copies)
        value = total(landing)
    return jnp.concatenate([value[:, :64], value[:, 64:]], axis=0)


def theta_scratch(tag):
    shapes = {}
    for name, size in SIZES.items():
        shapes[f"{tag}_{name}"] = pltpu.VMEM((size, 32, LANES), F32)
        shapes[f"{tag}_{name}_s"] = DMA((size,))
        shapes[f"{tag}_{name}_r"] = DMA((size,))
    return shapes


STAGES = ("xc", "y", "z", "y", "xc")


def mix_scratch(tag, rows):
    r = rows // NROW
    big, mid = (PLANE, DEEP, r, LANES), (DEEP, r, LANES)
    shapes = {
        f"{tag}_{n}": pltpu.VMEM(s, F32)
        for n, s in enumerate((big, big, mid, mid, (NCOL, r, LANES), mid, big))
    }
    for n, name in enumerate(STAGES):
        shapes[f"{tag}_s{n}"] = DMA((SIZES[name],))
        shapes[f"{tag}_r{n}"] = DMA((SIZES[name],))
    return shapes


def mix(place, rows, flat, refs, tag):
    r = rows // NROW
    data, land_a, half, land_b, land_z, back, result = (refs[f"{tag}_{n}"] for n in range(7))
    sems = [(refs[f"{tag}_s{n}"], refs[f"{tag}_r{n}"]) for n in range(5)]
    mine = {name: place.groups[name][1] for name in SIZES}
    for a in range(PLANE):
        for b in range(DEEP):
            at = (a * DEEP + b) * r
            data[a, b] = flat[at : at + r, :]
    land_a[mine["xc"]] = data[mine["xc"]]
    copies = swap(place, "xc", lambda peer: data.at[peer], land_a, *sems[0])
    yield
    finish(copies)
    half[...] = total(land_a)
    land_b[mine["y"]] = half[mine["y"]]
    copies = swap(place, "y", lambda peer: half.at[peer], land_b, *sems[1])
    yield
    finish(copies)
    land_z[mine["z"]] = total(land_b)
    copies = swap(place, "z", lambda peer: land_z.at[mine["z"]], land_z, *sems[2])
    yield
    finish(copies)
    back[mine["y"]] = total(land_z)
    copies = swap(place, "y", lambda peer: back.at[mine["y"]], back, *sems[3])
    yield
    finish(copies)
    result[mine["xc"]] = back[...]
    copies = swap(place, "xc", lambda peer: result.at[mine["xc"]], result, *sems[4])
    yield
    finish(copies)
    for a in range(PLANE):
        for b in range(DEEP):
            at = (a * DEEP + b) * r
            flat[at : at + r, :] = result[a, b]
    yield


def short_scratch(tag, rows):
    r = rows // PLANE
    shapes = {
        f"{tag}_{n}": pltpu.VMEM((size, r, LANES), F32)
        for n, size in enumerate((PLANE, PLANE, DEEP, NCOL, PLANE))
    }
    for n, name in enumerate(("xc", "y", "z", "xc")):
        shapes[f"{tag}_s{n}"] = DMA((SIZES[name],))
        shapes[f"{tag}_r{n}"] = DMA((SIZES[name],))
    return shapes


def mix_short(place, rows, flat, refs, tag):
    r = rows // PLANE
    data, land_a, land_b, land_z, result = (refs[f"{tag}_{n}"] for n in range(5))
    sems = [(refs[f"{tag}_s{n}"], refs[f"{tag}_r{n}"]) for n in range(4)]
    mine = {name: place.groups[name][1] for name in SIZES}
    for a in range(PLANE):
        data[a] = flat[a * r : (a + 1) * r, :]
    land_a[mine["xc"]] = data[mine["xc"]]
    copies = swap(place, "xc", lambda peer: data.at[peer], land_a, *sems[0])
    yield
    finish(copies)
    land_b[mine["y"]] = total(land_a)
    copies = swap(place, "y", lambda peer: land_b.at[mine["y"]], land_b, *sems[1])
    yield
    finish(copies)
    land_z[mine["z"]] = total(land_b)
    copies = swap(place, "z", lambda peer: land_z.at[mine["z"]], land_z, *sems[2])
    yield
    finish(copies)
    result[mine["xc"]] = total(land_z)
    copies = swap(place, "xc", lambda peer: result.at[mine["xc"]], result, *sems[3])
    yield
    finish(copies)
    for a in range(PLANE):
        flat[a * r : (a + 1) * r, :] = result[a]
    yield


def ring_scratch(tag):
    return {
        f"{tag}_held": pltpu.VMEM((NCOL, STRIPS, MODES, LANES), F32),
        f"{tag}_s": DMA((2, HOPS)),
        f"{tag}_r": DMA((2, HOPS)),
    }


def ring(place, refs, tag, spread_ref, first, each):
    held, sends, recvs = refs[f"{tag}_held"], refs[f"{tag}_s"], refs[f"{tag}_r"]
    per = STRIPS // PARTS
    devices = (place.right, place.left)

    def region(way, n, hop):
        q, s = n // PARTS, lax.rem(n, PARTS)
        if way == 0:
            return lax.rem(place.j + 2 * NCOL - q - hop, NCOL), s
        return lax.rem(place.j + q + hop, NCOL), PARTS - 1 - s

    def copy(way, n, hop=0):
        slot, part = region(way, n, hop)
        piece = held.at[slot, pl.ds(part * per, per)]
        return pltpu.make_async_remote_copy(
            src_ref=piece,
            dst_ref=piece,
            send_sem=sends.at[way, n],
            recv_sem=recvs.at[way, n],
            device_id=devices[way],
            device_id_type=MESH,
        )

    def spread(slot, first, count):
        def one(b, carry):
            value = held[slot, first + b]
            high = value.astype(BF16).astype(F32)
            at = 2 * (slot * STRIPS + first + b) + 1
            both = jnp.concatenate([high, value - high], axis=0).T.astype(BF16)
            spread_ref[at] = both[:TILE]
            spread_ref[at + 1] = both[TILE:]
            return carry

        lax.fori_loop(0, count, one, 0)

    def begin(n, carry):
        for way in range(2):
            copy(way, n).start()
        return carry

    def step(n, carry):
        for way in range(2):
            copy(way, n, 1).wait_recv()

            @pl.when(n + PARTS < HOPS)
            def forward():
                copy(way, n + PARTS).start()

        for way in range(2):
            slot, part = region(way, n, 1)
            spread(slot, part * per, per)
        each(n)
        return carry

    def end(n, carry):
        for way in range(2):
            copy(way, n).wait_send()
        return carry

    lax.fori_loop(0, PARTS, begin, 0)
    first()
    spread(place.j, 0, STRIPS)
    lax.fori_loop(0, HOPS, step, 0)
    lax.fori_loop(0, HOPS, end, 0)


def line(ref):
    value = ref[...].reshape(1, SLOTS)
    return jnp.concatenate([value, jnp.zeros((1, RANKS - SLOTS), I32)], axis=1)


def upright(value):
    return jnp.broadcast_to(value, (LANES, RANKS)).T


def count_of(where, value=1):
    return jnp.sum(jnp.where(where, value, 0), axis=0, keepdims=True)


def order(rows, cols, live):
    lane = lax.broadcasted_iota(I32, (1, RANKS), 1)
    row = jnp.where(lane < live, rows, 255)
    below = lax.broadcasted_iota(I32, (RANKS, LANES), 0)
    row_up = upright(row)
    rank = []
    for b in range(RANKS // LANES):
        here = lax.broadcasted_iota(I32, (RANKS, LANES), 1) + b * LANES
        same = (row_up == row[:, b * LANES : (b + 1) * LANES]) & (below < here)
        rank.append(count_of(same))
    rank = jnp.concatenate(rank, axis=1)
    name = lax.broadcasted_iota(I32, (RANKS, LANES), 1)
    held = count_of(row_up == name)
    pairs = jnp.right_shift(held + 1, 1)
    pairs_up = jnp.broadcast_to(pairs, (LANES, LANES)).T[:ROWS]
    named = lax.broadcasted_iota(I32, (ROWS, RANKS), 0)
    wide_pairs = jnp.concatenate([pairs_up] * (RANKS // LANES), axis=1)
    start = count_of(named < row, wide_pairs)
    place = jnp.where(lane < live, 2 * start + rank, 5000)
    code = lane + 1024 * (cols + 1) + jnp.where(rank == 0, FRESH, 0)
    place_up, code_up = upright(place), upright(code)
    found = []
    for b in range(RANKS // LANES):
        here = lax.broadcasted_iota(I32, (RANKS, LANES), 1) + b * LANES
        found.append(count_of(place_up == here, code_up))
    mine = lax.broadcasted_iota(I32, (ROWS, LANES), 0)
    at = lax.broadcasted_iota(I32, (ROWS, LANES), 1)
    ends = jnp.where(pairs > 0, count_of(mine <= at, pairs_up), 0)
    return jnp.concatenate(found, axis=1), ends


def pack_pair(p, codes, tiles, packed):
    half = jnp.right_shift(lax.broadcasted_iota(I32, (TILE, LANES), 1), 6)

    def one(place, wanted):
        slot = jnp.bitwise_and(codes[0, place], 1023)
        value = tiles[:, pl.ds(jnp.right_shift(slot, 1) * LANES, LANES)]
        odd = jnp.broadcast_to(jnp.bitwise_and(slot, 1), (TILE, LANES))
        return jnp.where(odd == wanted, value, pltpu.roll(value, TILE, 1))

    both = jnp.where(half == 0, one(2 * p, 0), one(2 * p + 1, 1))
    packed[p] = jnp.concatenate(halves(both), axis=1)


def multiply(codes, ends, packed, spread_ref, sums, part, after):
    def batch(s, run):
        found = []
        for u in range(BATCH):
            p = s * BATCH + u
            pair = (codes[0, 2 * p], codes[0, 2 * p + 1])
            tables = []
            for code in pair:
                tables.append(spread_ref[jnp.bitwise_and(jnp.right_shift(code, 10), 255)])
            out = jnp.dot(
                packed[p], jnp.concatenate(tables * 2, axis=0), preferred_element_type=F32
            )
            fresh = jnp.broadcast_to(pair[0], (TILE, LANES)) >= FRESH
            found.append((p, fresh, out))
        for p, fresh, out in found:
            run = jnp.where(fresh, 0.0, run) + out
            sums[p + 1] = run
        return run

    sums[0] = jnp.zeros((TILE, LANES), F32)
    lax.fori_loop(0, PAIRS // BATCH, batch, jnp.zeros((TILE, LANES), F32))

    def place(b, carry):
        both = jnp.concatenate([sums[ends[0, 2 * b]], sums[ends[0, 2 * b + 1]]], axis=0).T
        part[:, pl.ds(pl.multiple_of(b * LANES, LANES), LANES)] = both[:MODES] + both[MODES:]
        return carry

    for third in (0, 2, 1):
        lax.fori_loop(third * STRIPS, (third + 1) * STRIPS, place, 0)
        after(third)


def correct(place, x, ax, diag, theta_t, w, held):
    for s in range(STRIPS):
        at = slice(s * LANES, (s + 1) * LANES)
        value = (ax[:, at] - product(theta_t, x[:, at], NN)) / diag[:, at]
        w[:, at] = value
        held[place.j, s] = value


def theta_local(x, ax):
    return product(ax[...], x[...], NT) * (1.0 / DOFS)


def fold(value):
    return jnp.concatenate([value[:96], value[96:]], axis=1)


def unfold(value):
    return jnp.concatenate([value[:, :64], value[:, 64:]], axis=0)


def gram_rest(x, w, p, ax, ap, flat, base):
    basis = jnp.concatenate([x[...], w[...], p[...]], axis=0)
    other = jnp.concatenate([ax[...], ap[...], basis], axis=0)
    block = product(basis, other, NT) * (1.0 / DOFS)
    flat[base : base + 192, :] = block[:, :128]
    flat[base + 192 : base + 384, :] = block[:, 128:256]
    flat[base + 384 : base + 480, :] = fold(block[:, 256:])


def gram_image(x, w, p, aw, flat):
    basis = jnp.concatenate([x[...], w[...], p[...]], axis=0)
    flat[0:96, :] = fold(product(basis, aw[...], NT) * (1.0 / DOFS))


def halo_scratch(tag):
    return {
        f"{tag}_above": pltpu.VMEM((MODES, LOCAL), F32),
        f"{tag}_below": pltpu.VMEM((MODES, LOCAL), F32),
        f"{tag}_s": DMA((2,)),
        f"{tag}_r": DMA((2,)),
    }


def halo(place, part, refs, tag, third):
    at = third // 2
    copy = pltpu.make_async_remote_copy(
        src_ref=part.at[:, pl.ds(third * LOCAL, LOCAL)],
        dst_ref=refs[f"{tag}_below" if at else f"{tag}_above"],
        send_sem=refs[f"{tag}_s"].at[at],
        recv_sem=refs[f"{tag}_r"].at[at],
        device_id=place.next_row if at else place.last_row,
        device_id_type=MESH,
    )
    copy.start()
    return copy


def image(part, w, diag, refs, tag, aw):
    aw[...] = (
        part[:, LOCAL : 2 * LOCAL]
        + refs[f"{tag}_below"][...]
        + refs[f"{tag}_above"][...]
        + diag[...] * w[...]
    )


def rotate(turn, x, w, p, next_x, next_p):
    moved = product(turn[:, 64:], jnp.concatenate([w[...], p[...]], axis=0), NN)
    next_p[...] = moved
    next_x[...] = product(turn[:, :64], x[...], NN) + moved


def put_grams(rest, image_block, grams, k):
    block = rest[0:192]
    grams[k, 0] = jnp.concatenate([block[:, :64], unfold(image_block), block[:, 64:]], axis=1)
    grams[k, 1] = jnp.concatenate([rest[192:384], unfold(rest[384:480])], axis=1)


FIELDS = ("x", "ax", "diag", "p", "ap")
FIELD = pltpu.VMEM((MODES, LOCAL), F32)
NAMED = Scratch(
    {name: FIELD for name in FIELDS}
    | {f"{n}{k}": FIELD for k in (1, 2) for n in ("x", "p", "ax", "ap")}
    | {name: FIELD for name in ("w", "w1", "aw", "aw1")}
    | {
        "turn": pltpu.VMEM((2, MODES, 3 * MODES), F32),
        "tiles": pltpu.VMEM((TILE, SLOTS * TILE), F32),
        "loads": DMA((7,)),
        "stores": DMA((6,)),
        "codes_v": pltpu.VMEM((1, RANKS), I32),
        "ends_v": pltpu.VMEM((1, LANES), I32),
        "codes": pltpu.SMEM((1, RANKS), I32),
        "ends": pltpu.SMEM((1, LANES), I32),
        "lists": DMA((2,)),
        "packed": pltpu.VMEM((PAIRS, TILE, 2 * LANES), BF16),
        "sums": pltpu.VMEM((PAIRS + 1, TILE, LANES), F32),
        "spread": pltpu.VMEM((BLOCKS + 1, TILE, LANES), BF16),
        "part": pltpu.VMEM((MODES, 3 * LOCAL), F32),
        "flat0": pltpu.VMEM((480, LANES), F32),
        "flat1": pltpu.VMEM((576, LANES), F32),
        "flat2": pltpu.VMEM((96, LANES), F32),
        "grams": pltpu.VMEM((2, 2, 192, 192), F32),
    }
    | theta_scratch("theta0")
    | theta_scratch("theta1")
    | ring_scratch("ring0")
    | ring_scratch("ring1")
    | halo_scratch("halo0")
    | halo_scratch("halo1")
    | mix_scratch("mix0", 480)
    | mix_scratch("mix1", 576)
    | short_scratch("mix2", 96)
)
BESIDE_Y, BESIDE_Z = 72, 200


def steps(
    rows, cols, count, x_in, ax_in, diag_in, p_in, ap_in, turn_in, tiles_in,
    x_out, p_out, ax_out, ap_out, grams_out, *refs,
):
    place = Place()
    ready = greet(place, rows=True)
    r = NAMED.found(refs)
    loads = {}
    for n, (name, source) in enumerate(
        zip(FIELDS + ("turn", "tiles"), (x_in, ax_in, diag_in, p_in, ap_in, turn_in, tiles_in))
    ):
        loads[name] = pltpu.make_async_copy(source, r[name], r["loads"].at[n])
        loads[name].start()
    stores = []

    def store(source, target):
        copy = pltpu.make_async_copy(source, target, r["stores"].at[len(stores)])
        copy.start()
        stores.append(copy)

    codes, ends, packed, tiles = r["codes"], r["ends"], r["packed"], r["tiles"]
    x, ax, diag, p, ap = (r[name] for name in FIELDS)
    w, w1, aw, aw1, part, spread_ref = (
        r[n] for n in ("w", "w1", "aw", "aw1", "part", "spread")
    )

    def nothing(*unused):
        pass

    def sort():
        code, end = order(line(rows), line(cols), count[0])
        r["codes_v"][...] = code
        r["ends_v"][...] = end
        moves = [
            pltpu.make_async_copy(r["codes_v"], codes, r["lists"].at[0]),
            pltpu.make_async_copy(r["ends_v"], ends, r["lists"].at[1]),
        ]
        for move in moves:
            move.start()
        for move in moves:
            move.wait()
        spread_ref[0] = jnp.zeros((TILE, LANES), BF16)

    def pack(a, b):
        def four(s, carry):
            for u in range(4):
                pack_pair(4 * s + u, codes, tiles, packed)
            return carry

        return lambda: lax.fori_loop(a // 4, b // 4, four, 0)

    def pack_first():
        loads["tiles"].wait()
        pack(0, BESIDE_Y)()

    loads["x"].wait()
    loads["ax"].wait()
    local = theta_local(x, ax)
    ready()
    theta_t = sum_theta(
        place, local, r, "theta0", (sort, pack_first, pack(BESIDE_Y, BESIDE_Z))
    )
    loads["diag"].wait()
    correct(place, x, ax, diag, theta_t, w, r["ring0_held"])
    loads["p"].wait()
    loads["ap"].wait()
    loads["turn"].wait()
    mix0 = mix(place, 480, r["flat0"], r, "mix0")
    mix1 = mix(place, 576, r["flat1"], r, "mix1")
    mix2 = mix_short(place, 96, r["flat2"], r, "mix2")

    def first0():
        gram_rest(x, w, p, ax, ap, r["flat0"], 0)
        next(mix0)

    def each0(n):
        for u in range(8):
            pack_pair(BESIDE_Z + n * 8 + u, codes, tiles, packed)

    ring(place, r, "ring0", spread_ref, first0, each0)
    next(mix0)
    sent = []

    def send(tag):
        return lambda third: third == 1 or sent.append(halo(place, part, r, tag, third))

    multiply(codes, ends, packed, spread_ref, r["sums"], part, send("halo0"))
    next(mix0)
    x1, p1, ax1, ap1 = (r[n] for n in ("x1", "p1", "ax1", "ap1"))
    rotate(r["turn"][0], x, w, p, x1, p1)
    finish(sent)
    image(part, w, diag, r, "halo0", aw)
    rotate(r["turn"][0], ax, aw, ap, ax1, ap1)
    theta_t = sum_theta(
        place,
        theta_local(x1, ax1),
        r,
        "theta1",
        (nothing, lambda: gram_image(x, w, p, aw, r["flat1"]), lambda: next(mix0)),
    )
    correct(place, x1, ax1, diag, theta_t, w1, r["ring1_held"])

    def first1():
        gram_rest(x1, w1, p1, ax1, ap1, r["flat1"], 96)
        next(mix1)

    ring(place, r, "ring1", spread_ref, first1, nothing)
    next(mix1)
    next(mix0)
    sent = []
    multiply(codes, ends, packed, spread_ref, r["sums"], part, send("halo1"))
    next(mix1)
    x2, p2, ax2, ap2 = (r[n] for n in ("x2", "p2", "ax2", "ap2"))
    rotate(r["turn"][1], x1, w1, p1, x2, p2)
    store(x2, x_out)
    store(p2, p_out)
    finish(sent)
    image(part, w1, diag, r, "halo1", aw1)
    gram_image(x1, w1, p1, aw1, r["flat2"])
    next(mix2)
    next(mix1)
    rotate(r["turn"][1], ax1, aw1, ap1, ax2, ap2)
    store(ax2, ax_out)
    store(ap2, ap_out)
    next(mix2)
    next(mix1)
    next(mix0)
    next(mix2)
    next(mix1)
    put_grams(r["flat0"][...], r["flat1"][0:96], r["grams"], 0)
    store(r["grams"].at[0], grams_out.at[0])
    next(mix2)
    next(mix2)
    put_grams(r["flat1"][96:576], r["flat2"][...], r["grams"], 1)
    store(r["grams"].at[1], grams_out.at[1])
    for copy in stores:
        copy.wait()


def body(x, p, ax, ap, diag, tiles, rows, cols, count, turns):
    field = jax.ShapeDtypeStruct((MODES, LOCAL), F32)
    far = pl.BlockSpec(memory_space=pl.ANY)
    found = pl.pallas_call(
        steps,
        out_shape=[field] * 4 + [jax.ShapeDtypeStruct((2, 2, 192, 192), F32)],
        in_specs=[
            pl.BlockSpec(memory_space=pltpu.VMEM),
            pl.BlockSpec(memory_space=pltpu.VMEM),
            pl.BlockSpec(memory_space=pltpu.SMEM),
        ]
        + [far] * 7,
        out_specs=[far] * 5,
        scratch_shapes=NAMED.shapes,
        compiler_params=pltpu.CompilerParams(
            collective_id=1, has_side_effects=True, vmem_limit_bytes=60 << 20
        ),
        name="steps",
    )(rows, cols, count, x, ax, diag, p, ap, turns.swapaxes(1, 2), tiles)
    return pl.pallas_call(
        hand_over,
        out_shape=[jax.ShapeDtypeStruct(f.shape, f.dtype) for f in found],
        in_specs=[far] * 5,
        out_specs=[far] * 5,
        scratch_shapes=[pltpu.VMEM(f.shape, f.dtype) for f in found] + [DMA((5,))] * 2,
        compiler_params=pltpu.CompilerParams(vmem_limit_bytes=60 << 20),
        name="hand_over",
    )(*found)


def hand_over(*refs):
    given, wanted, held, (inward, outward) = refs[:5], refs[5:10], refs[10:15], refs[15:]
    first = [pltpu.make_async_copy(given[n], held[n], inward.at[n]) for n in range(5)]
    last = [pltpu.make_async_copy(held[n], wanted[n], outward.at[n]) for n in range(5)]
    for copy in first:
        copy.start()
    for n in range(5):
        first[n].wait()
        last[n].start()
    for copy in last:
        copy.wait()


def solution(mesh):
    split = P(None, ("row", "col"))
    listed = P(("row", "col"))
    return jax.shard_map(
        lambda *args: tuple(body(*args)),
        mesh=mesh,
        in_specs=(split,) * 6 + (listed,) * 3 + (P(),),
        out_specs=(split,) * 4 + (P(),),
        check_vma=False,
    )
```

time: 173 us -> 129 us (0.75)
  Pallas kernels: 159 us -> 127 us
  local copies, waits for them, and re-layouts: 12.4 us -> 0 us
    pallas_call x5 -> x2, Pallas kernels: 159 us -> 127 us  [the longest x1 125 us: body(): pl.pallas_call(steps, out_shape=[field] * 4 + [jax.ShapeDtypeStruct((2, 2...]
    unnamed x28 -> x0, local copies, waits for them, and re-layouts: 12.4 us -> none
where the time goes in v2:
time: 129 us; the launch traced here: 128 us
  Pallas kernels  127 us (98%)
  between operations  1.29 us (1%)
    pallas_call x1, Pallas kernels, body(): pl.pallas_call(steps, out_shape=[field] * 4 + [jax.ShapeDtypeStruct((2, 2...  125 us

profile of v2, /device:TPU:1, one launch (start us, length us, event | category | flops | bytes accessed | tf_op | source)
XLA Modules:
  0.0 128.4 jit_solution(539336672177246159)
XLA Ops:
  1.3 124.7 %steps.1 = (f32[64,1024]{1,0:T(8,128)}, f32[64,1024]{1,0:T(8,128)}, f32[64,1024]{1,0:T(8,128)}, f32[64,1024]{1,0:T(8,128)}, f32[2,2,192,192]{3,2,1,0:T(8,128)}) custom-call(s32[576]{0:T(1024)} %rows.1, s32[576]{0:T(1024)} %cols.1, s32[1]{0:T(128)S(6)} %copy.15.count, f32[64,1024]{1,0:T(8,128)} %x_in.1, f32[64,1024]{1,0:T(8,128)} %ax_in.1, ...), custom_call_target="tpu_custom_call" | custom-call | tf_op jit(solution)/shard_map/steps/pallas_call | solution.py:660
  126.0 2.4 %hand_over.1 = (f32[64,1024]{1,0:T(8,128)}, f32[64,1024]{1,0:T(8,128)}, f32[64,1024]{1,0:T(8,128)}, f32[64,1024]{1,0:T(8,128)}, f32[2,2,192,192]{3,2,1,0:T(8,128)}) custom-call(f32[64,1024]{1,0:T(8,128)} %get-tuple-element.10.refs_0_, f32[64,1024]{1,0:T(8,128)} %get-tuple-element.11.refs_1_, f32[64,1024]{1,0:T(8,128)} %get-tuple-element.12.refs_2_, ...), custom_call_target="tpu_custom_call" | custom-call | tf_op jit(solution)/shard_map/hand_over/pallas_call | solution.py:676

commit v3 on v2

--- a/solution.py
+++ b/solution.py
@@ -25,6 +25,7 @@
 ROWS = 3 * BPD
 PARTS = 4
 HOPS = 3 * PARTS + PARTS // 2
+PER = STRIPS // PARTS
 RANKS = 640
 PAIRS = SLOTS // 2 + ROWS // 2
 BATCH = 24
@@ -244,70 +245,69 @@
     }
 
 
-def ring(place, refs, tag, spread_ref, first, each):
-    held, sends, recvs = refs[f"{tag}_held"], refs[f"{tag}_s"], refs[f"{tag}_r"]
-    per = STRIPS // PARTS
-    devices = (place.right, place.left)
-
-    def region(way, n, hop):
+class Ring:
+    def __init__(self, place, refs, tag, spread_ref):
+        self.place, self.spread_ref = place, spread_ref
+        self.held, self.sends, self.recvs = (refs[f"{tag}_{n}"] for n in ("held", "s", "r"))
+        self.devices = (place.right, place.left)
+
+    def region(self, way, n, hop):
         q, s = n // PARTS, lax.rem(n, PARTS)
         if way == 0:
-            return lax.rem(place.j + 2 * NCOL - q - hop, NCOL), s
-        return lax.rem(place.j + q + hop, NCOL), PARTS - 1 - s
-
-    def copy(way, n, hop=0):
-        slot, part = region(way, n, hop)
-        piece = held.at[slot, pl.ds(part * per, per)]
+            return lax.rem(self.place.j + 2 * NCOL - q - hop, NCOL), s
+        return lax.rem(self.place.j + q + hop, NCOL), lax.rem(s + PARTS // 2, PARTS)
+
+    def copy(self, way, n, hop=0):
+        slot, part = self.region(way, n, hop)
+        piece = self.held.at[slot, pl.ds(part * PER, PER)]
         return pltpu.make_async_remote_copy(
             src_ref=piece,
             dst_ref=piece,
-            send_sem=sends.at[way, n],
-            recv_sem=recvs.at[way, n],
-            device_id=devices[way],
+            send_sem=self.sends.at[way, n],
+            recv_sem=self.recvs.at[way, n],
+            device_id=self.devices[way],
             device_id_type=MESH,
         )
 
-    def spread(slot, first, count):
+    def spread(self, slot, first, count):
         def one(b, carry):
-            value = held[slot, first + b]
+            value = self.held[slot, first + b]
             high = value.astype(BF16).astype(F32)
             at = 2 * (slot * STRIPS + first + b) + 1
             both = jnp.concatenate([high, value - high], axis=0).T.astype(BF16)
-            spread_ref[at] = both[:TILE]
-            spread_ref[at + 1] = both[TILE:]
+            self.spread_ref[at] = both[:TILE]
+            self.spread_ref[at + 1] = both[TILE:]
             return carry
 
         lax.fori_loop(0, count, one, 0)
 
-    def begin(n, carry):
-        for way in range(2):
-            copy(way, n).start()
-        return carry
-
-    def step(n, carry):
-        for way in range(2):
-            copy(way, n, 1).wait_recv()
-
-            @pl.when(n + PARTS < HOPS)
-            def forward():
-                copy(way, n + PARTS).start()
-
-        for way in range(2):
-            slot, part = region(way, n, 1)
-            spread(slot, part * per, per)
-        each(n)
-        return carry
-
-    def end(n, carry):
-        for way in range(2):
-            copy(way, n).wait_send()
-        return carry
-
-    lax.fori_loop(0, PARTS, begin, 0)
-    first()
-    spread(place.j, 0, STRIPS)
-    lax.fori_loop(0, HOPS, step, 0)
-    lax.fori_loop(0, HOPS, end, 0)
+    def run(self, tasks, each):
+        def step(n, carry):
+            for way in range(2):
+                self.copy(way, n, 1).wait_recv()
+
+                @pl.when(n + PARTS < HOPS)
+                def forward():
+                    self.copy(way, n + PARTS).start()
+
+            for way in range(2):
+                slot, part = self.region(way, n, 1)
+                self.spread(slot, part * PER, PER)
+            each(n)
+            return carry
+
+        def end(n, carry):
+            for way in range(2):
+                self.copy(way, n).wait_send()
+            return carry
+
+        done = 0
+        for stop, task in tasks:
+            lax.fori_loop(done, stop, step, 0)
+            task()
+            done = stop
+        lax.fori_loop(done, HOPS, step, 0)
+        lax.fori_loop(0, HOPS, end, 0)
 
 
 def line(ref):
@@ -399,12 +399,17 @@
         after(third)
 
 
-def correct(place, x, ax, diag, theta_t, w, held):
-    for s in range(STRIPS):
-        at = slice(s * LANES, (s + 1) * LANES)
-        value = (ax[:, at] - product(theta_t, x[:, at], NN)) / diag[:, at]
-        w[:, at] = value
-        held[place.j, s] = value
+def correct(place, x, ax, diag, theta_t, w, ring):
+    for part, way, n in ((0, 0, 0), (2, 1, 0), (1, 0, 1), (3, 1, 1)):
+        for s in range(part * PER, (part + 1) * PER):
+            at = slice(s * LANES, (s + 1) * LANES)
+            value = (ax[:, at] - product(theta_t, x[:, at], NN)) / diag[:, at]
+            w[:, at] = value
+            ring.held[place.j, s] = value
+        ring.copy(way, n).start()
+    for n in (2, 3):
+        for way in range(2):
+            ring.copy(way, n).start()
 
 
 def theta_local(x, ax):
@@ -454,6 +459,28 @@
     )
     copy.start()
     return copy
+
+
+def near_scratch():
+    shapes = {f"near_{n}": pltpu.VMEM((2, MODES, LOCAL), F32) for n in "xpw"}
+    return shapes | {"near_s": DMA((6,)), "near_r": DMA((6,))}
+
+
+def lend(place, refs, name, field):
+    copies = []
+    for side, device in enumerate((place.next_row, place.last_row)):
+        at = 2 * "xpw".index(name) + side
+        copy = pltpu.make_async_remote_copy(
+            src_ref=field,
+            dst_ref=refs[f"near_{name}"].at[side],
+            send_sem=refs["near_s"].at[at],
+            recv_sem=refs["near_r"].at[at],
+            device_id=device,
+            device_id_type=MESH,
+        )
+        copy.start()
+        copies.append(copy)
+    return copies
 
 
 def image(part, w, diag, refs, tag, aw):
@@ -502,6 +529,8 @@
         "flat2": pltpu.VMEM((96, LANES), F32),
         "grams": pltpu.VMEM((2, 2, 192, 192), F32),
     }
+    | {"before_t": pltpu.VMEM((MODES, MODES), F32), "before_g": pltpu.VMEM((192, MODES), F32)}
+    | near_scratch()
     | theta_scratch("theta0")
     | theta_scratch("theta1")
     | ring_scratch("ring0")
@@ -578,77 +607,122 @@
         place, local, r, "theta0", (sort, pack_first, pack(BESIDE_Y, BESIDE_Z))
     )
     loads["diag"].wait()
-    correct(place, x, ax, diag, theta_t, w, r["ring0_held"])
+    ring = Ring(place, r, "ring0", spread_ref)
+    correct(place, x, ax, diag, theta_t, w, ring)
     loads["p"].wait()
     loads["ap"].wait()
     loads["turn"].wait()
-    mix0 = mix(place, 480, r["flat0"], r, "mix0")
-    mix1 = mix(place, 576, r["flat1"], r, "mix1")
-    mix2 = mix_short(place, 96, r["flat2"], r, "mix2")
-
-    def first0():
-        gram_rest(x, w, p, ax, ap, r["flat0"], 0)
+    flat0, flat1, flat2, before_t, before_g = (
+        r[n] for n in ("flat0", "flat1", "flat2", "before_t", "before_g")
+    )
+    x1, p1, ax1, ap1 = (r[n] for n in ("x1", "p1", "ax1", "ap1"))
+    x2, p2, ax2, ap2 = (r[n] for n in ("x2", "p2", "ax2", "ap2"))
+    near_x, near_p, near_w = (r[f"near_{n}"] for n in "xpw")
+    mix0 = mix(place, 480, flat0, r, "mix0")
+    mix1 = mix(place, 576, flat1, r, "mix1")
+    mix2 = mix_short(place, 96, flat2, r, "mix2")
+    lent, sent = [], []
+
+    def thirds(n):
+        return part[:, n * LOCAL : (n + 1) * LOCAL]
+
+    def own0():
+        ring.spread(place.j, 0, STRIPS)
+        gram_rest(x, w, p, ax, ap, flat0, 0)
         next(mix0)
+
+    def turn0():
+        rotate(r["turn"][0], x, w, p, x1, p1)
+        lent.extend(lend(place, r, "x", x1))
+        lent.extend(lend(place, r, "p", p1))
+
+    def theta0():
+        known = jnp.concatenate([ax[...], diag[...] * w[...], ap[...]], axis=0)
+        before_t[...] = product(product(r["turn"][0], known, NN), x1[...], NT)
 
     def each0(n):
         for u in range(8):
             pack_pair(BESIDE_Z + n * 8 + u, codes, tiles, packed)
 
-    ring(place, r, "ring0", spread_ref, first0, each0)
-    next(mix0)
-    sent = []
-
     def send(tag):
         return lambda third: third == 1 or sent.append(halo(place, part, r, tag, third))
 
+    ring.run(((0, own0), (3, turn0), (6, lambda: next(mix0)), (8, theta0)), each0)
+    next(mix0)
     multiply(codes, ends, packed, spread_ref, r["sums"], part, send("halo0"))
     next(mix0)
-    x1, p1, ax1, ap1 = (r[n] for n in ("x1", "p1", "ax1", "ap1"))
-    rotate(r["turn"][0], x, w, p, x1, p1)
-    finish(sent)
-    image(part, w, diag, r, "halo0", aw)
-    rotate(r["turn"][0], ax, aw, ap, ax1, ap1)
+    finish(lent)
+    core = (
+        product(thirds(0), near_x[0], NT)
+        + product(thirds(2), near_x[1], NT)
+        + product(thirds(1), x1[...], NT)
+    )
+    local = before_t[...] + product(r["turn"][0][:, 64:128], core, NN)
+
+    def images0():
+        finish(sent)
+        image(part, w, diag, r, "halo0", aw)
+        rotate(r["turn"][0], ax, aw, ap, ax1, ap1)
+
+    def grams0():
+        gram_image(x, w, p, aw, flat1)
+
     theta_t = sum_theta(
-        place,
-        theta_local(x1, ax1),
-        r,
-        "theta1",
-        (nothing, lambda: gram_image(x, w, p, aw, r["flat1"]), lambda: next(mix0)),
-    )
-    correct(place, x1, ax1, diag, theta_t, w1, r["ring1_held"])
-
-    def first1():
-        gram_rest(x1, w1, p1, ax1, ap1, r["flat1"], 96)
+        place, local * (1.0 / DOFS), r, "theta1", (nothing, images0, grams0)
+    )
+    ring = Ring(place, r, "ring1", spread_ref)
+    correct(place, x1, ax1, diag, theta_t, w1, ring)
+    lent, sent = [], []
+
+    def own1():
+        lent.extend(lend(place, r, "w", w1))
+        ring.spread(place.j, 0, STRIPS)
+        gram_rest(x1, w1, p1, ax1, ap1, flat1, 96)
         next(mix1)
 
-    ring(place, r, "ring1", spread_ref, first1, nothing)
+    def turn1():
+        rotate(r["turn"][1], x1, w1, p1, x2, p2)
+        store(x2, x_out)
+        store(p2, p_out)
+
+    def image1():
+        basis = jnp.concatenate([x1[...], w1[...], p1[...]], axis=0)
+        before_g[...] = product(basis, diag[...] * w1[...], NT)
+
+    def both():
+        next(mix0)
+        next(mix1)
+
+    ring.run(
+        ((0, own1), (3, turn1), (5, lambda: next(mix0)), (7, image1), (9, both)), nothing
+    )
     next(mix1)
-    next(mix0)
-    sent = []
     multiply(codes, ends, packed, spread_ref, r["sums"], part, send("halo1"))
     next(mix1)
-    x2, p2, ax2, ap2 = (r[n] for n in ("x2", "p2", "ax2", "ap2"))
-    rotate(r["turn"][1], x1, w1, p1, x2, p2)
-    store(x2, x_out)
-    store(p2, p_out)
+    finish(lent)
+    total_image = before_g[...]
+    for third, fields in (
+        (0, (near_x[0], near_w[0], near_p[0])),
+        (1, (x1[...], w1[...], p1[...])),
+        (2, (near_x[1], near_w[1], near_p[1])),
+    ):
+        total_image += product(jnp.concatenate(fields, axis=0), thirds(third), NT)
+    flat2[...] = fold(total_image * (1.0 / DOFS))
+    next(mix2)
+    next(mix2)
     finish(sent)
     image(part, w1, diag, r, "halo1", aw1)
-    gram_image(x1, w1, p1, aw1, r["flat2"])
     next(mix2)
     next(mix1)
     rotate(r["turn"][1], ax1, aw1, ap1, ax2, ap2)
     store(ax2, ax_out)
     store(ap2, ap_out)
-    next(mix2)
     next(mix1)
-    next(mix0)
-    next(mix2)
-    next(mix1)
-    put_grams(r["flat0"][...], r["flat1"][0:96], r["grams"], 0)
+    put_grams(flat0[...], flat1[0:96], r["grams"], 0)
     store(r["grams"].at[0], grams_out.at[0])
     next(mix2)
     next(mix2)
-    put_grams(r["flat1"][96:576], r["flat2"][...], r["grams"], 1)
+    put_grams(flat1[96:576], flat2[...], r["grams"], 1)
     store(r["grams"].at[1], grams_out.at[1])
     for copy in stores:
         copy.wait()

time: 129 us -> 122 us (0.946)
  Pallas kernels: 127 us -> 121 us
    pallas_call x1, Pallas kernels: 125 us -> 118 us  [body(): pl.pallas_call(steps, out_shape=[field] * 4 + [jax.ShapeDtypeStruct((2, 2...]
where the time goes in v3:
time: 122 us
  Pallas kernels  121 us (99%)
  between operations  1.29 us (1%)
    pallas_call x1, Pallas kernels, body(): pl.pallas_call(steps, out_shape=[field] * 4 + [jax.ShapeDtypeStruct((2, 2...  118 us

profile of v3, /device:TPU:1, one launch (start us, length us, event | category | flops | bytes accessed | tf_op | source)
XLA Modules:
  0.0 122.0 jit_solution(12430251026681090108)
XLA Ops:
  1.3 118.3 %steps.1 = (f32[64,1024]{1,0:T(8,128)}, f32[64,1024]{1,0:T(8,128)}, f32[64,1024]{1,0:T(8,128)}, f32[64,1024]{1,0:T(8,128)}, f32[2,2,192,192]{3,2,1,0:T(8,128)}) custom-call(s32[576]{0:T(1024)} %rows.1, s32[576]{0:T(1024)} %cols.1, s32[1]{0:T(128)S(6)} %copy.15.count, f32[64,1024]{1,0:T(8,128)} %x_in.1, f32[64,1024]{1,0:T(8,128)} %ax_in.1, ...), custom_call_target="tpu_custom_call" | custom-call | tf_op jit(solution)/shard_map/steps/pallas_call | solution.py:734
  119.6 2.4 %hand_over.1 = (f32[64,1024]{1,0:T(8,128)}, f32[64,1024]{1,0:T(8,128)}, f32[64,1024]{1,0:T(8,128)}, f32[64,1024]{1,0:T(8,128)}, f32[2,2,192,192]{3,2,1,0:T(8,128)}) custom-call(f32[64,1024]{1,0:T(8,128)} %get-tuple-element.10.refs_0_, f32[64,1024]{1,0:T(8,128)} %get-tuple-element.11.refs_1_, f32[64,1024]{1,0:T(8,128)} %get-tuple-element.12.refs_2_, ...), custom_call_target="tpu_custom_call" | custom-call | tf_op jit(solution)/shard_map/hand_over/pallas_call | solution.py:750

commit v4 on v3

--- a/solution.py
+++ b/solution.py
@@ -28,7 +28,7 @@
 PER = STRIPS // PARTS
 RANKS = 640
 PAIRS = SLOTS // 2 + ROWS // 2
-BATCH = 24
+BATCH = 78
 FRESH = 1 << 18
 
 
@@ -395,7 +395,7 @@
         return carry
 
     for third in (0, 2, 1):
-        lax.fori_loop(third * STRIPS, (third + 1) * STRIPS, place, 0)
+        lax.fori_loop(third * STRIPS, (third + 1) * STRIPS, place, 0, unroll=STRIPS)
         after(third)
 
 
@@ -498,9 +498,12 @@
     next_x[...] = product(turn[:, :64], x[...], NN) + moved
 
 
-def put_grams(rest, image_block, grams, k):
+def put_stiff(rest, image_block, grams, k):
     block = rest[0:192]
     grams[k, 0] = jnp.concatenate([block[:, :64], unfold(image_block), block[:, 64:]], axis=1)
+
+
+def put_mass(rest, grams, k):
     grams[k, 1] = jnp.concatenate([rest[192:384], unfold(rest[384:480])], axis=1)
 
 
@@ -514,7 +517,7 @@
         "turn": pltpu.VMEM((2, MODES, 3 * MODES), F32),
         "tiles": pltpu.VMEM((TILE, SLOTS * TILE), F32),
         "loads": DMA((7,)),
-        "stores": DMA((6,)),
+        "stores": DMA((7,)),
         "codes_v": pltpu.VMEM((1, RANKS), I32),
         "ends_v": pltpu.VMEM((1, LANES), I32),
         "codes": pltpu.SMEM((1, RANKS), I32),
@@ -718,12 +721,15 @@
     store(ax2, ax_out)
     store(ap2, ap_out)
     next(mix1)
-    put_grams(flat0[...], flat1[0:96], r["grams"], 0)
+    put_stiff(flat0[...], flat1[0:96], r["grams"], 0)
+    put_mass(flat0[...], r["grams"], 0)
     store(r["grams"].at[0], grams_out.at[0])
+    put_mass(flat1[96:576], r["grams"], 1)
+    store(r["grams"].at[1, 1], grams_out.at[1, 1])
     next(mix2)
     next(mix2)
-    put_grams(flat1[96:576], flat2[...], r["grams"], 1)
-    store(r["grams"].at[1], grams_out.at[1])
+    put_stiff(flat1[96:576], flat2[...], r["grams"], 1)
+    store(r["grams"].at[1, 0], grams_out.at[1, 0])
     for copy in stores:
         copy.wait()
 

time: 122 us -> 117 us (0.959)
  Pallas kernels: 121 us -> 116 us
    pallas_call x1, Pallas kernels: 118 us -> 113 us  [body(): pl.pallas_call(steps, out_shape=[field] * 4 + [jax.ShapeDtypeStruct((2, 2...]
where the time goes in v4:
time: 117 us
  Pallas kernels  116 us (99%)
  between operations  1.45 us (1%)
    pallas_call x1, Pallas kernels, body(): pl.pallas_call(steps, out_shape=[field] * 4 + [jax.ShapeDtypeStruct((2, 2...  113 us
    pallas_call x1, Pallas kernels, body(): pl.pallas_call(hand_over, out_shape=[jax.ShapeDtypeStruct(f.shape, f.dtyp...  2.42 us

profile of v4, /device:TPU:1, one launch (start us, length us, event | category | flops | bytes accessed | tf_op | source)
XLA Modules:
  0.0 117.3 jit_solution(15301552539468720965)
XLA Ops:
  1.3 113.4 %steps.1 = (f32[64,1024]{1,0:T(8,128)}, f32[64,1024]{1,0:T(8,128)}, f32[64,1024]{1,0:T(8,128)}, f32[64,1024]{1,0:T(8,128)}, f32[2,2,192,192]{3,2,1,0:T(8,128)}) custom-call(s32[576]{0:T(1024)} %rows.1, s32[576]{0:T(1024)} %cols.1, s32[1]{0:T(128)S(6)} %copy.15.count, f32[64,1024]{1,0:T(8,128)} %x_in.1, f32[64,1024]{1,0:T(8,128)} %ax_in.1, ...), custom_call_target="tpu_custom_call" | custom-call | tf_op jit(solution)/shard_map/steps/pallas_call | solution.py:740
  114.7 2.4 %hand_over.1 = (f32[64,1024]{1,0:T(8,128)}, f32[64,1024]{1,0:T(8,128)}, f32[64,1024]{1,0:T(8,128)}, f32[64,1024]{1,0:T(8,128)}, f32[2,2,192,192]{3,2,1,0:T(8,128)}) custom-call(f32[64,1024]{1,0:T(8,128)} %get-tuple-element.10.refs_0_, f32[64,1024]{1,0:T(8,128)} %get-tuple-element.11.refs_1_, f32[64,1024]{1,0:T(8,128)} %get-tuple-element.12.refs_2_, ...), custom_call_target="tpu_custom_call" | custom-call | tf_op jit(solution)/shard_map/hand_over/pallas_call | solution.py:756

commit v5 on v4

--- a/solution.py
+++ b/solution.py
@@ -28,7 +28,7 @@
 PER = STRIPS // PARTS
 RANKS = 640
 PAIRS = SLOTS // 2 + ROWS // 2
-BATCH = 78
+BATCH = 156
 FRESH = 1 << 18
 
 
@@ -38,11 +38,14 @@
 
 
 def product(a, b, dims):
+    return split_product(halves(a), halves(b), dims)
+
+
+def split_product(a, b, dims):
     dot = functools.partial(
         lax.dot_general, dimension_numbers=(dims, ((), ())), preferred_element_type=F32
     )
-    a_high, a_low = halves(a)
-    b_high, b_low = halves(b)
+    (a_high, a_low), (b_high, b_low) = a, b
     return dot(a_high, b_high) + (dot(a_high, b_low) + dot(a_low, b_high))
 
 
@@ -533,6 +536,7 @@
         "grams": pltpu.VMEM((2, 2, 192, 192), F32),
     }
     | {"before_t": pltpu.VMEM((MODES, MODES), F32), "before_g": pltpu.VMEM((192, MODES), F32)}
+    | {f"s_{n}": pltpu.VMEM((3, 3 * MODES, LOCAL), BF16) for n in ("high", "low")}
     | near_scratch()
     | theta_scratch("theta0")
     | theta_scratch("theta1")
@@ -621,6 +625,7 @@
     x1, p1, ax1, ap1 = (r[n] for n in ("x1", "p1", "ax1", "ap1"))
     x2, p2, ax2, ap2 = (r[n] for n in ("x2", "p2", "ax2", "ap2"))
     near_x, near_p, near_w = (r[f"near_{n}"] for n in "xpw")
+    s_high, s_low = r["s_high"], r["s_low"]
     mix0 = mix(place, 480, flat0, r, "mix0")
     mix1 = mix(place, 576, flat1, r, "mix1")
     mix2 = mix_short(place, 96, flat2, r, "mix2")
@@ -646,6 +651,12 @@
     def each0(n):
         for u in range(8):
             pack_pair(BESIDE_Z + n * 8 + u, codes, tiles, packed)
+
+    def keep(high, low, third, fields):
+        high[third], low[third] = halves(jnp.concatenate(fields, axis=0))
+
+    def kept(high, low, third):
+        return (high[third], low[third]), halves(thirds(third))
 
     def send(tag):
         return lambda third: third == 1 or sent.append(halo(place, part, r, tag, third))
@@ -666,12 +677,10 @@
         finish(sent)
         image(part, w, diag, r, "halo0", aw)
         rotate(r["turn"][0], ax, aw, ap, ax1, ap1)
-
-    def grams0():
         gram_image(x, w, p, aw, flat1)
 
     theta_t = sum_theta(
-        place, local * (1.0 / DOFS), r, "theta1", (nothing, images0, grams0)
+        place, local * (1.0 / DOFS), r, "theta1", (nothing, nothing, images0)
     )
     ring = Ring(place, r, "ring1", spread_ref)
     correct(place, x1, ax1, diag, theta_t, w1, ring)
@@ -692,31 +701,33 @@
         basis = jnp.concatenate([x1[...], w1[...], p1[...]], axis=0)
         before_g[...] = product(basis, diag[...] * w1[...], NT)
 
+    def keep1():
+        finish(lent)
+        keep(s_high, s_low, 0, [near_x[0], near_w[0], near_p[0]])
+        keep(s_high, s_low, 1, [x1[...], w1[...], p1[...]])
+        keep(s_high, s_low, 2, [near_x[1], near_w[1], near_p[1]])
+
     def both():
         next(mix0)
         next(mix1)
 
     ring.run(
-        ((0, own1), (3, turn1), (5, lambda: next(mix0)), (7, image1), (9, both)), nothing
+        ((0, own1), (3, turn1), (5, lambda: next(mix0)), (7, image1), (9, both), (11, keep1)),
+        nothing,
     )
     next(mix1)
     multiply(codes, ends, packed, spread_ref, r["sums"], part, send("halo1"))
     next(mix1)
-    finish(lent)
-    total_image = before_g[...]
-    for third, fields in (
-        (0, (near_x[0], near_w[0], near_p[0])),
-        (1, (x1[...], w1[...], p1[...])),
-        (2, (near_x[1], near_w[1], near_p[1])),
-    ):
-        total_image += product(jnp.concatenate(fields, axis=0), thirds(third), NT)
+    total_image = before_g[...] + sum(
+        split_product(*kept(s_high, s_low, n), NT) for n in range(3)
+    )
     flat2[...] = fold(total_image * (1.0 / DOFS))
     next(mix2)
     next(mix2)
+    next(mix2)
+    next(mix1)
     finish(sent)
     image(part, w1, diag, r, "halo1", aw1)
-    next(mix2)
-    next(mix1)
     rotate(r["turn"][1], ax1, aw1, ap1, ax2, ap2)
     store(ax2, ax_out)
     store(ap2, ap_out)

time: 117 us -> 117 us (level)
  no operation moved by 1% of the time
where the time goes in v5:
time: 117 us
  Pallas kernels  115 us (98%)
  between operations  1.45 us (1%)
    pallas_call x1, Pallas kernels, body(): pl.pallas_call(steps, out_shape=[field] * 4 + [jax.ShapeDtypeStruct((2, 2...  113 us
    pallas_call x1, Pallas kernels, body(): pl.pallas_call(hand_over, out_shape=[jax.ShapeDtypeStruct(f.shape, f.dtyp...  2.42 us

profile of v5, /device:TPU:1, one launch (start us, length us, event | category | flops | bytes accessed | tf_op | source)
XLA Modules:
  0.0 116.8 jit_solution(3326343977284886751)
XLA Ops:
  1.3 112.9 %steps.1 = (f32[64,1024]{1,0:T(8,128)}, f32[64,1024]{1,0:T(8,128)}, f32[64,1024]{1,0:T(8,128)}, f32[64,1024]{1,0:T(8,128)}, f32[2,2,192,192]{3,2,1,0:T(8,128)}) custom-call(s32[576]{0:T(1024)} %rows.1, s32[576]{0:T(1024)} %cols.1, s32[1]{0:T(128)S(6)} %copy.15.count, f32[64,1024]{1,0:T(8,128)} %x_in.1, f32[64,1024]{1,0:T(8,128)} %ax_in.1, ...), custom_call_target="tpu_custom_call" | custom-call | tf_op jit(solution)/shard_map/steps/pallas_call | solution.py:751
  114.2 2.4 %hand_over.1 = (f32[64,1024]{1,0:T(8,128)}, f32[64,1024]{1,0:T(8,128)}, f32[64,1024]{1,0:T(8,128)}, f32[64,1024]{1,0:T(8,128)}, f32[2,2,192,192]{3,2,1,0:T(8,128)}) custom-call(f32[64,1024]{1,0:T(8,128)} %get-tuple-element.10.refs_0_, f32[64,1024]{1,0:T(8,128)} %get-tuple-element.11.refs_1_, f32[64,1024]{1,0:T(8,128)} %get-tuple-element.12.refs_2_, ...), custom_call_target="tpu_custom_call" | custom-call | tf_op jit(solution)/shard_map/hand_over/pallas_call | solution.py:767
